TPU v7x, 32 devices: a whole 2x2x4 slice. The times are simulated.
32 devices in a mesh: groups: 2 (over x), tensor: 4 (over y, core), adapter: 4 (over z).
Axes of the slice: x: 2, y: 2, z: 4, core: 2. Of those that a mesh axis runs over, the one named last changes fastest.
Arguments:
- tokens: bfloat16 [2048, 8192], P(('groups', 'adapter'), 'tensor'), parts along dimension 0, may hold values from -6 to 6
- tenant: int32 [2048, 1], P(('groups', 'adapter')), parts along dimension 0, may hold values from 0 to 7; in each aligned block of 256 rows (0 to 255, 256 to 511, ...) at most 96 rows name the same one
- adapter_storage_rows: int32 [16], P('groups'), parts along dimension 0, may hold values from 0 to 7, each once
- frozen_projection_weight: bfloat16 [8192, 8192], P('tensor'), may hold values from -0.09375 to 0.09375
- shrink_factor_matrices: float32 [16, 64, 8192], P(('groups', 'adapter'), None, 'tensor'), parts along dimension 0, may hold values from -0.0625 to 0.0625
- expand_factor_matrices: float32 [16, 64, 8192], P(('groups', 'adapter'), None, 'tensor'), parts along dimension 0, may hold values from -0.0625 to 0.0625
- shrink_running_mean: float32 [16, 64, 8192], P(('groups', 'adapter'), None, 'tensor'), parts along dimension 0, may hold values from -6 to 6
- expand_running_mean: float32 [16, 64, 8192], P(('groups', 'adapter'), None, 'tensor'), parts along dimension 0, may hold values from -6 to 6
- shrink_running_variance: float32 [16, 64, 8192], P(('groups', 'adapter'), None, 'tensor'), parts along dimension 0, may hold values from 0.25 to 4
- expand_running_variance: float32 [16, 64, 8192], P(('groups', 'adapter'), None, 'tensor'), parts along dimension 0, may hold values from 0.25 to 4
- output_gradient: bfloat16 [2048, 8192], P(('groups', 'adapter'), 'tensor'), parts along dimension 0, may hold values from -6 to 6
Outputs:
- layer_result: bfloat16 [2048, 8192], P(('groups', 'adapter'), 'tensor'), parts along dimension 0
- input_sensitivity: bfloat16 [2048, 8192], P(('groups', 'adapter'), 'tensor'), parts along dimension 0
- revised_shrink_factor: float32 [16, 64, 8192], P(('groups', 'adapter'), None, 'tensor'), parts along dimension 0
- revised_expand_factor: float32 [16, 64, 8192], P(('groups', 'adapter'), None, 'tensor'), parts along dimension 0
- revised_shrink_mean: float32 [16, 64, 8192], P(('groups', 'adapter'), None, 'tensor'), parts along dimension 0
- revised_expand_mean: float32 [16, 64, 8192], P(('groups', 'adapter'), None, 'tensor'), parts along dimension 0
- revised_shrink_variance: float32 [16, 64, 8192], P(('groups', 'adapter'), None, 'tensor'), parts along dimension 0
- revised_expand_variance: float32 [16, 64, 8192], P(('groups', 'adapter'), None, 'tensor'), parts along dimension 0
There are 2 independent parts, one for each index of `groups`. A program takes and returns all parts, laid end to end along the dimension named above; an argument that names none is the same for every part. Nothing has to cross between parts.
Inputs may be any that keep to these rules, and one draw needn't show every extreme that they name: `tenant`: among the 256 tokens of one index of adapter (aligned blocks of rows) no adapter id appears more than 96 times, and in at least one block some id appears exactly 96 times. `adapter_storage_rows`: A permutation: each storage row holds exactly one adapter.
All inputs are finite; a program needn't handle non-finite values.
Results may differ from a plain program's by a relative error of at most 0.013.
Values may be sent and summed in bfloat16 or wider, within the bound.
A program may use at most 192 MiB of HBM per device.

v0:
```python
import jax
import jax.numpy as jnp
from jax import lax
from jax.sharding import PartitionSpec as P

beta_one = 0.9
beta_two = 0.999
learn_rate = 0.01
adam_eps = 1e-08
adam_step = 10
adapter_scale = 2.0


def optimizer_advance(param, grad, first, second):
    first_next = beta_one * first + (1.0 - beta_one) * grad
    second_next = beta_two * second + (1.0 - beta_two) * grad * grad
    fix_one = 1.0 - beta_one**adam_step
    fix_two = 1.0 - beta_two**adam_step
    param_next = param - learn_rate * (first_next / fix_one) / (
        jnp.sqrt(second_next / fix_two) + adam_eps
    )
    return (param_next, first_next, second_next)


def on_device(
    tokens,
    tenant,
    adapter_storage_rows,
    frozen_projection_weight,
    shrink_factor_matrices,
    expand_factor_matrices,
    shrink_running_mean,
    expand_running_mean,
    shrink_running_variance,
    expand_running_variance,
    output_gradient,
):
    f32 = jnp.float32
    brain_float_half = jnp.bfloat16
    tok_rows, width_dev = tokens.shape
    count_adapters = adapter_storage_rows.shape[0]
    capacity = 3 * tok_rows // count_adapters
    slots = count_adapters * capacity
    labels = lax.broadcasted_iota(jnp.int32, (1, count_adapters), 1)
    chosen = (tenant == labels).astype(jnp.int32)
    stored = jnp.sum(chosen * adapter_storage_rows[None, :], axis=1)
    by_row = (stored[:, None] == labels).astype(jnp.int32)
    before = jnp.cumsum(by_row, axis=0) - by_row
    rank_in = jnp.sum(before * by_row, axis=1)
    target = stored * capacity + rank_in
    placing = (lax.broadcasted_iota(jnp.int32, (slots, tok_rows), 0) == target[None, :]).astype(
        brain_float_half
    )
    x_slots = jnp.dot(placing, tokens, preferred_element_type=f32).astype(brain_float_half)
    dy_slots = jnp.dot(placing, output_gradient, preferred_element_type=f32).astype(
        brain_float_half
    )
    down_maps_half = shrink_factor_matrices.astype(brain_float_half)
    up_maps_half = expand_factor_matrices.astype(brain_float_half)
    all_down, all_up = (
        lax.all_gather(down_maps_half, "adapter", axis=0, tiled=True),
        lax.all_gather(up_maps_half, "adapter", axis=0, tiled=True),
    )
    x_rows = x_slots.reshape(count_adapters, capacity, width_dev)
    dy_rows = dy_slots.reshape(count_adapters, capacity, width_dev)
    low_part = jnp.einsum("acd,ard->acr", x_rows, all_down, preferred_element_type=f32)
    back_part = jnp.einsum("acd,ard->acr", dy_rows, all_up, preferred_element_type=f32)
    lowrank_activation_sum, backward_lowrank_sum = lax.psum((low_part, back_part), "tensor")
    lowrank_activation_half = (adapter_scale * lowrank_activation_sum).astype(brain_float_half)
    backward_lowrank_half = (adapter_scale * backward_lowrank_sum).astype(brain_float_half)
    delta_flat = (
        jnp.einsum("acr,ard->acd", lowrank_activation_half, all_up, preferred_element_type=f32)
        .astype(brain_float_half)
        .reshape(slots, width_dev)
    )
    back_flat = (
        jnp.einsum("acr,ard->acd", backward_lowrank_half, all_down, preferred_element_type=f32)
        .astype(brain_float_half)
        .reshape(slots, width_dev)
    )
    terms_down = jnp.einsum(
        "acr,acd->ard", backward_lowrank_half, x_rows, preferred_element_type=f32
    )
    terms_up = jnp.einsum(
        "acr,acd->ard", lowrank_activation_half, dy_rows, preferred_element_type=f32
    )
    shrink_factor_cotangent, expand_factor_cotangent = (
        lax.psum_scatter(
            terms_down.astype(jnp.bfloat16), "adapter", scatter_dimension=0, tiled=True
        ).astype(jnp.float32),
        lax.psum_scatter(
            terms_up.astype(jnp.bfloat16), "adapter", scatter_dimension=0, tiled=True
        ).astype(jnp.float32),
    )
    delta_tok = lax.dot_general(
        placing, delta_flat, (((0,), (0,)), ((), ())), preferred_element_type=f32
    )
    back_tok = lax.dot_general(
        placing, back_flat, (((0,), (0,)), ((), ())), preferred_element_type=f32
    )
    partial_value = jnp.dot(tokens, frozen_projection_weight, preferred_element_type=f32)
    base_out = lax.psum_scatter(partial_value, "tensor", scatter_dimension=1, tiled=True)
    layer_result = (base_out + delta_tok).astype(brain_float_half)
    base_back = lax.dot_general(
        lax.all_gather(output_gradient, "tensor", axis=1, tiled=True),
        frozen_projection_weight,
        (((1,), (1,)), ((), ())),
        preferred_element_type=f32,
    )
    input_sensitivity = (base_back + back_tok).astype(brain_float_half)
    revised_shrink_factor, revised_shrink_mean, revised_shrink_variance = optimizer_advance(
        shrink_factor_matrices,
        shrink_factor_cotangent,
        shrink_running_mean,
        shrink_running_variance,
    )
    revised_expand_factor, revised_expand_mean, revised_expand_variance = optimizer_advance(
        expand_factor_matrices,
        expand_factor_cotangent,
        expand_running_mean,
        expand_running_variance,
    )
    return (
        layer_result,
        input_sensitivity,
        revised_shrink_factor,
        revised_expand_factor,
        revised_shrink_mean,
        revised_expand_mean,
        revised_shrink_variance,
        revised_expand_variance,
    )


def solution(mesh):
    return jax.shard_map(
        on_device,
        mesh=mesh,
        in_specs=(
            P(("groups", "adapter"), "tensor"),
            P(("groups", "adapter"), None),
            P("groups"),
            P("tensor", None),
            P(("groups", "adapter"), None, "tensor"),
            P(("groups", "adapter"), None, "tensor"),
            P(("groups", "adapter"), None, "tensor"),
            P(("groups", "adapter"), None, "tensor"),
            P(("groups", "adapter"), None, "tensor"),
            P(("groups", "adapter"), None, "tensor"),
            P(("groups", "adapter"), "tensor"),
        ),
        out_specs=(
            P(("groups", "adapter"), "tensor"),
            P(("groups", "adapter"), "tensor"),
            P(("groups", "adapter"), None, "tensor"),
            P(("groups", "adapter"), None, "tensor"),
            P(("groups", "adapter"), None, "tensor"),
            P(("groups", "adapter"), None, "tensor"),
            P(("groups", "adapter"), None, "tensor"),
            P(("groups", "adapter"), None, "tensor"),
        ),
        check_vma=False,
    )
```

profile of v0, /device:TPU:15, one launch (start us, length us, event | category | flops | bytes accessed | tf_op | source)
XLA Modules:
  0.0 352.3 jit_solution(4745040967869496662)
XLA Ops:
  7.2 0.0 copy-start
  7.2 0.0 copy-start.12
  7.2 0.0 copy-start.11
  7.2 0.0 all-gather.4.cloned.1.call-start
  7.3 2.2 convert_element_type.54
  9.4 0.0 all-gather.4.cloned.1.call-update
  9.4 0.0 all-gather.6.cloned.1.call-start
  9.5 2.1 convert_element_type.56
  11.6 0.0 all-gather.6.cloned.1.call-update
  11.6 0.0 all-reduce.3.cloned.1.call-start
  11.6 0.0 copy-done.12
  11.7 0.0 copy-done.11
  11.7 0.1 select_reduce_fusion
  11.8 0.6 reduce-window.6
  12.3 0.2 slice_reduce_fusion
  12.6 0.1 fusion.11
  12.7 0.0 copy-done
  12.7 0.0 copy-start.5
  12.7 2.7 convolution_convert_fusion.3
  15.4 0.0 copy-done.5
  15.4 2.6 convolution_convert_fusion.2
  18.0 37.4 %all-gather.4.cloned.1.call-done = bf16[8,64,2048]{2,1,0:T(8,128)(2,1)} async-done(((bf16[2,64,2048]{2,1,0:T(8,128)(2,1)}), bf16[8,64,2048]{2,1,0:T(8,128)(2,1)}) %all-gather.4.cloned.1.call-update) | async-done | bytes 2097168 | tf_op jit(solution)/shard_map/all_gather | solution.py:61
  55.4 4.5 %fusion.22 = f32[8,96,64]{1,2,0:T(8,128)} fusion(bf16[8,96,2048]{2,1,0:T(8,128)(2,1)} %bitcast.32, bf16[8,64,2048]{2,1,0:T(8,128)(2,1)} %all-gather.4.cloned.1.call-done), kind=kOutput, calls=%fused_computation.42 | convolution fusion | flops 201326592 | bytes 5439488 | tf_op jit(solution)/shard_map/acd,ard->acr/dot_general | solution.py:66
  59.9 42.3 %all-gather.6.cloned.1.call-done = bf16[8,64,2048]{2,1,0:T(8,128)(2,1)} async-done(((bf16[2,64,2048]{2,1,0:T(8,128)(2,1)}), bf16[8,64,2048]{2,1,0:T(8,128)(2,1)}) %all-gather.6.cloned.1.call-update) | async-done | bytes 2097168 | tf_op jit(solution)/shard_map/all_gather | solution.py:62
  102.2 4.5 %fusion.24 = f32[8,96,64]{1,2,0:T(8,128)} fusion(bf16[8,96,2048]{2,1,0:T(8,128)(2,1)} %bitcast.30, bf16[8,64,2048]{2,1,0:T(8,128)(2,1)} %all-gather.6.cloned.1.call-done), kind=kOutput, calls=%fused_computation.44 | convolution fusion | flops 201326592 | bytes 5439488 | tf_op jit(solution)/shard_map/acd,ard->acr/dot_general | solution.py:67
  106.7 0.0 all-reduce.3.cloned.1.call-update
  106.7 0.0 all-gather.8.cloned.1.call-start
  106.8 0.5 all-gather.8.cloned.1.call-update
  107.3 0.0 reduce-scatter.6.cloned.1.call-start
  107.4 31.5 %all-reduce.3.cloned.1.call-done = (f32[8,96,64]{1,2,0:T(8,128)}, f32[8,96,64]{1,2,0:T(8,128)}) async-done(((f32[8,96,64]{1,2,0:T(8,128)}, f32[8,96,64]{1,2,0:T(8,128)}), (f32[8,96,64]{1,2,0:T(8,128)}, f32[8,96,64]{1,2,0:T(8,128)})) %all-reduce.3.cloned.1.call-update) | async-done | bytes 393232 | tf_op jit(solution)/shard_map/psum | solution.py:68
  138.8 0.0 copy-start.10
  138.8 4.0 %convolution_convert_fusion.5 = bf16[8,64,2048]{2,1,0:T(8,128)(2,1)} fusion(bf16[8,96,2048]{2,1,0:T(8,128)(2,1)} %bitcast.33, f32[8,96,64]{1,2,0:T(8,128)} %get-tuple-element.9), kind=kOutput, calls=%fused_computation.5 | convolution fusion | flops 202473472 | bytes 5439488 | tf_op jit(solution)/shard_map/acr,acd->ard/dot_general | solution.py:81
  142.9 0.0 reduce-scatter.6.cloned.1.call-update
  142.9 0.0 reduce-scatter.8.cloned.1.call-start
  142.9 0.0 copy-done.10
  143.0 3.9 %convolution_convert_fusion.4 = bf16[8,64,2048]{2,1,0:T(8,128)(2,1)} fusion(bf16[8,96,2048]{2,1,0:T(8,128)(2,1)} %bitcast.31, f32[8,96,64]{1,2,0:T(8,128)S(1)} %copy-done.10), kind=kOutput, calls=%fused_computation.4 | convolution fusion | flops 202473472 | bytes 5439488 | tf_op jit(solution)/shard_map/acr,acd->ard/dot_general | solution.py:84
  146.9 0.0 reduce-scatter.8.cloned.1.call-update
  146.9 0.2 reduce-scatter.4.cloned.1.call-start
  147.1 18.5 %fusion.21 = f32[256,8192]{1,0:T(8,128)} fusion(bf16[256,2048]{1,0:T(8,128)(2,1)S(1)} %copy-done, bf16[2048,8192]{1,0:T(8,128)(2,1)} %param.14), kind=kOutput, calls=%fused_computation.41 | convolution fusion | flops 8589934592 | bytes 42991616 | tf_op jit(solution)/shard_map/dot_general | solution.py:101
  165.6 0.0 reduce-scatter.4.cloned.1.call-update
  165.7 1.6 copy-done.4
  167.3 0.0 copy-start.3
  167.3 0.0 copy-start.9
  167.3 2.6 convolution_convert_fusion.1
  169.9 0.0 copy-done.3
  169.9 0.0 copy-done.9
  169.9 2.7 convolution_convert_fusion
  172.6 3.5 all-gather.8.cloned.1.call-done
  176.1 0.0 copy-start.2
  176.1 17.6 %fusion.23 = f32[256,2048]{1,0:T(8,128)} fusion(bf16[256,8192]{1,0:T(8,128)(2,1)} %all-gather.8.cloned.1.call-done, bf16[2048,8192]{1,0:T(8,128)(2,1)} %param.14), kind=kOutput, calls=%fused_computation.43 | convolution fusion | flops 8589934592 | bytes 39845888 | tf_op jit(solution)/shard_map/dot_general | solution.py:104
  193.7 0.0 copy-done.2
  193.7 0.0 copy-start.6
  193.7 3.7 %fusion.1 = bf16[256,2048]{1,0:T(8,128)(2,1)} fusion(f32[256,2048]{1,0:T(8,128)} %fusion.23, bf16[768,2048]{1,0:T(8,128)(2,1)S(1)} %bitcast.35, s32[256]{0:T(256)S(1)} %multiply_add_fusion), kind=kOutput, calls=%fused_computation.9 | convolution fusion | flops 806551552 | bytes 6292480 | tf_op jit(solution)/shard_map/dot_general | solution.py:98
  197.4 0.0 copy-start.7
  197.4 22.9 %reduce-scatter.6.cloned.1.call-done = bf16[2,64,2048]{2,1,0:T(8,128)(2,1)} async-done(((bf16[8,64,2048]{2,1,0:T(8,128)(2,1)}), bf16[2,64,2048]{2,1,0:T(8,128)(2,1)}) %reduce-scatter.6.cloned.1.call-update) | async-done | bytes 524304 | tf_op jit(solution)/shard_map/reduce_scatter | solution.py:88
  220.2 0.0 copy-done.6
  220.2 3.8 %divide_subtract_fusion.1 = (f32[2,64,2048]{2,1,0:T(8,128)}, f32[2,64,2048]{2,1,0:T(8,128)}, f32[2,64,2048]{2,1,0:T(8,128)}) fusion(f32[2,64,2048]{2,1,0:T(8,128)S(1)} %copy-done.6, bf16[2,64,2048]{2,1,0:T(8,128)(2,1)} %reduce-scatter.6.cloned.1.call-done, f32[2,64,2048]{2,1,0:T(8,128)} %param.17, f32[2,64,2048]{2,1,0:T(8,128)} %param.19), kind=kLoop, calls=%fused_computation.19 | loop fusion | flops 3407872 | bytes 6815744 | tf_op jit(solution)/shard_map/sub | solution.py:19
  224.0 41.7 %reduce-scatter.8.cloned.1.call-done = bf16[2,64,2048]{2,1,0:T(8,128)(2,1)} async-done(((bf16[8,64,2048]{2,1,0:T(8,128)(2,1)}), bf16[2,64,2048]{2,1,0:T(8,128)(2,1)}) %reduce-scatter.8.cloned.1.call-update) | async-done | bytes 524304 | tf_op jit(solution)/shard_map/reduce_scatter | solution.py:91
  265.7 0.0 copy-done.7
  265.7 0.0 copy-done.8
  265.7 3.5 divide_subtract_fusion
  269.2 71.6 %reduce-scatter.4.cloned.1.call-done = f32[256,2048]{1,0:T(8,128)} async-done(((f32[256,8192]{1,0:T(8,128)}), f32[256,2048]{1,0:T(8,128)}) %reduce-scatter.4.cloned.1.call-update) | async-done | bytes 2097168 | tf_op jit(solution)/shard_map/reduce_scatter | solution.py:102
  340.8 4.6 %fusion = bf16[256,2048]{1,0:T(8,128)(2,1)} fusion(f32[256,2048]{1,0:T(8,128)} %reduce-scatter.4.cloned.1.call-done, bf16[768,2048]{1,0:T(8,128)(2,1)} %bitcast.34, s32[256]{0:T(256)S(1)} %multiply_add_fusion), kind=kOutput, calls=%fused_computation.8 | convolution fusion | flops 806551552 | bytes 6292480 | tf_op jit(solution)/shard_map/dot_general | solution.py:95
  345.5 0.0 copy-done.1
  (7 shorter events, 0.1 us)
Async XLA Ops:
  7.2 5.5 %copy-start = (bf16[256,2048]{1,0:T(8,128)(2,1)S(1)}, bf16[256,2048]{1,0:T(8,128)(2,1)}, u32[]{:S(2)}) copy-start(bf16[256,2048]{1,0:T(8,128)(2,1)} %param.11) | copy-start | bytes 3145732
  7.2 4.5 %copy-start.12 = (s32[8]{0:T(128)S(1)}, s32[8]{0:T(128)}, u32[]{:S(2)}) copy-start(s32[8]{0:T(128)} %param.13) | copy-start | bytes 100
  7.2 4.5 %copy-start.11 = (s32[256,1]{0,1:T(1,128)S(1)}, s32[256,1]{0,1:T(1,128)}, u32[]{:S(2)}) copy-start(s32[256,1]{0,1:T(1,128)} %param.12) | copy-start | bytes 3076
  7.2 48.2 %all-gather.4.cloned.1.call-start = ((), (), s32[]{:S(2)}) async-start(), calls=%async_computation.4 | async-start | bytes 2621440 | tf_op jit(solution)/shard_map/all_gather | solution.py:61
  9.4 92.8 %all-gather.6.cloned.1.call-start = ((), (), s32[]{:S(2)}) async-start(), calls=%async_computation.5 | async-start | bytes 2621440 | tf_op jit(solution)/shard_map/all_gather | solution.py:62
  11.6 127.2 %all-reduce.3.cloned.1.call-start = ((), (), s32[]{:S(2)}) async-start(), calls=%async_computation.9 | async-start | bytes 1048576 | tf_op jit(solution)/shard_map/psum | solution.py:68
  12.7 2.7 copy-start.5
  106.7 69.4 %all-gather.8.cloned.1.call-start = ((), (), s32[]{:S(2)}) async-start(), calls=%async_computation.6 | async-start | bytes 5242880 | tf_op jit(solution)/shard_map/all_gather | solution.py:105
  107.3 112.9 %reduce-scatter.6.cloned.1.call-start = ((), (), s32[]{:S(2)}) async-start(), calls=%async_computation.7 | async-start | bytes 2621440 | tf_op jit(solution)/shard_map/reduce_scatter | solution.py:88
  138.8 4.1 %copy-start.10 = (f32[8,96,64]{1,2,0:T(8,128)S(1)}, f32[8,96,64]{1,2,0:T(8,128)}, u32[]{:S(2)}) copy-start(f32[8,96,64]{1,2,0:T(8,128)} %get-tuple-element.8) | copy-start | bytes 589828
  142.9 122.8 %reduce-scatter.8.cloned.1.call-start = ((), (), s32[]{:S(2)}) async-start(), calls=%async_computation.8 | async-start | bytes 2621440 | tf_op jit(solution)/shard_map/reduce_scatter | solution.py:91
  146.9 194.0 %reduce-scatter.4.cloned.1.call-start = ((), (), s32[]{:S(2)}) async-start(), calls=%async_computation.3 | async-start | bytes 10485760 | tf_op jit(solution)/shard_map/reduce_scatter | solution.py:102
  165.6 1.6 copy-start.4
  167.3 2.7 copy-start.3
  167.3 2.7 copy-start.9
  176.1 17.6 %copy-start.2 = (bf16[8,96,2048]{2,1,0:T(8,128)(2,1)S(1)}, bf16[8,96,2048]{2,1,0:T(8,128)(2,1)}, u32[]{:S(2)}) copy-start(bf16[8,96,2048]{2,1,0:T(8,128)(2,1)} %convolution_convert_fusion) | copy-start | bytes 9437188
  193.7 26.6 %copy-start.6 = (f32[2,64,2048]{2,1,0:T(8,128)S(1)}, f32[2,64,2048]{2,1,0:T(8,128)}, u32[]{:S(2)}) copy-start(f32[2,64,2048]{2,1,0:T(8,128)} %param.15) | copy-start | bytes 3145732
  197.4 68.4 %copy-start.7 = (f32[2,64,2048]{2,1,0:T(8,128)S(1)}, f32[2,64,2048]{2,1,0:T(8,128)}, u32[]{:S(2)}) copy-start(f32[2,64,2048]{2,1,0:T(8,128)} %param.16) | copy-start | bytes 3145732
  197.4 68.4 %copy-start.8 = (f32[2,64,2048]{2,1,0:T(8,128)S(1)}, f32[2,64,2048]{2,1,0:T(8,128)}, u32[]{:S(2)}) copy-start(f32[2,64,2048]{2,1,0:T(8,128)} %param.18) | copy-start | bytes 3145732
  340.8 4.6 %copy-start.1 = (bf16[256,2048]{1,0:T(8,128)(2,1)S(1)}, bf16[256,2048]{1,0:T(8,128)(2,1)}, u32[]{:S(2)}) copy-start(bf16[256,2048]{1,0:T(8,128)(2,1)} %param.11) | copy-start | bytes 3145732
Sparse Core Ops, SparseCore 0:
  10.2 45.1 all-gather.3
  57.5 44.6 all-gather.5
  106.9 31.9 all-reduce.2
  140.3 35.7 all-gather.7
  178.2 41.9 reduce-scatter.5
  222.5 43.1 reduce-scatter.7
  268.3 72.4 reduce-scatter.3
where the time goes:
time: 355 us; the launch traced here: 352 us
  waiting for transfers between devices  252 us (71%)
  matrix products  71.9 us (20%)
  between operations  14.2 us (4%)
  other arithmetic  12.3 us (3%)
    reduce_scatter x1, waiting for transfers between devices, on_device(): lax.psum_scatter(partial_value, 'tensor', scatter_dimension=1, tiled=True)  71.6 us
    all_gather x1, waiting for transfers between devices, on_device(): lax.all_gather(up_maps_half, 'adapter', axis=0, tiled=True)  42.3 us
    reduce_scatter x1, waiting for transfers between devices, on_device(): lax.psum_scatter(terms_up.astype(jnp.bfloat16), 'adapter', scatter_dimens...  41.7 us
    all_gather x1, waiting for transfers between devices, on_device(): lax.all_gather(down_maps_half, 'adapter', axis=0, tiled=True)  37.4 us
    psum x1, waiting for transfers between devices, on_device(): lax.psum((low_part, back_part), 'tensor')  31.5 us
    reduce_scatter x1, waiting for transfers between devices, on_device(): lax.psum_scatter(terms_down.astype(jnp.bfloat16), 'adapter', scatter_dime...  22.9 us
    dot_general x1, matrix products, on_device(): jnp.dot(tokens, frozen_projection_weight, preferred_element_type=f32)  18.5 us
    dot_general x1, matrix products, on_device(): lax.dot_general(lax.all_gather(output_gradient, 'tensor', axis=1, tiled=T...  17.6 us
  transfers between devices with their start and end apart: 7, of which 7 were waited for; matrix products, arithmetic and copies ran while one was open for 21% of the time, Pallas kernels for 0%

commit v1 on v0

v1 whole, which is shorter than its diff:
```python
import jax
import jax.numpy as jnp
from jax import lax
from jax.sharding import PartitionSpec as P

beta_one = 0.9
beta_two = 0.999
learn_rate = 0.01
adam_eps = 1e-08
adam_step = 10
adapter_scale = 2.0
f32 = jnp.float32
half = jnp.bfloat16


def optimizer_advance(param, grad, first, second):
    first_next = beta_one * first + (1.0 - beta_one) * grad
    second_next = beta_two * second + (1.0 - beta_two) * grad * grad
    fix_one = 1.0 - beta_one**adam_step
    fix_two = 1.0 - beta_two**adam_step
    param_next = param - learn_rate * (first_next / fix_one) / (
        jnp.sqrt(second_next / fix_two) + adam_eps
    )
    return (param_next, first_next, second_next)


def swap(value, size, bit):
    return lax.ppermute(value, "tensor", [(i, i ^ bit) for i in range(size)])


def bits_down(size):
    bit = size // 2
    while bit:
        yield bit
        bit //= 2


def tensor_gather(value, size, me):
    rows, width = value.shape
    held = value[:, None, :]
    for bit in bits_down(size):
        other = swap(held, size, bit)
        high = (me & bit) != 0
        held = jnp.stack(
            [jnp.where(high, other, held), jnp.where(high, held, other)], axis=2
        ).reshape(rows, -1, width)
    return held.reshape(rows, size * width)


def tensor_scatter(value, size, me):
    rows = value.shape[0]
    held = value.reshape(rows, size, -1)
    width = held.shape[2]
    bit = 1
    total = held
    while bit < size:
        pairs = total.reshape(rows, -1, 2, width)
        mine = ((me & bit) != 0).astype(jnp.int32)
        keep = lax.dynamic_index_in_dim(pairs, mine, 2, keepdims=False)
        give = lax.dynamic_index_in_dim(pairs, 1 - mine, 2, keepdims=False)
        other = swap(give.astype(half), size, bit)
        total = keep.astype(f32) + other.astype(f32)
        bit *= 2
    return total.reshape(rows, width)


def tensor_sum(value, size):
    if size == 4:
        a, b, c = (swap(value, size, k) for k in (1, 2, 3))
        return (value + a) + (b + c)
    bit = 1
    while bit < size:
        value = value + swap(value, size, bit)
        bit *= 2
    return value


def chain_gather(own, size, me, after=None):
    left, right = [own], [own]
    for t in range(1, size):
        left.append(
            lax.ppermute(left[-1], "adapter", [(i, i + 1) for i in range(t - 1, size - 1)])
        )
        right.append(
            lax.ppermute(right[-1], "adapter", [(i, i - 1) for i in range(1, size - t + 1)])
        )
    slots = [own] + [jnp.where(me >= t, left[t], right[size - t]) for t in range(1, size)]
    return jnp.concatenate(slots, axis=0), left, right


def chain_scatter(terms, size):
    from_left = from_right = None
    for d in range(size - 1, 0, -1):
        rightward, leftward = terms[size - d], terms[d]
        if from_left is not None:
            rightward = rightward + from_left.astype(f32)
            leftward = leftward + from_right.astype(f32)
        from_left = lax.ppermute(
            rightward.astype(half), "adapter", [(i, i + 1) for i in range(size - d)]
        )
        from_right = lax.ppermute(
            leftward.astype(half), "adapter", [(i, i - 1) for i in range(d, size)]
        )
    total = terms[0]
    if from_left is not None:
        total = total + from_left.astype(f32) + from_right.astype(f32)
    return total


def make(n_tensor, n_adapter):
    def on_device(
        tokens,
        tenant,
        adapter_storage_rows,
        frozen_projection_weight,
        shrink_factor_matrices,
        expand_factor_matrices,
        shrink_running_mean,
        expand_running_mean,
        shrink_running_variance,
        expand_running_variance,
        output_gradient,
    ):
        count = adapter_storage_rows.shape[0]
        own, rank, width = shrink_factor_matrices.shape
        zi, ti = lax.axis_index("adapter"), lax.axis_index("tensor")
        down_own = shrink_factor_matrices.reshape(own * rank, width).astype(half)
        up_own = expand_factor_matrices.reshape(own * rank, width).astype(half)

        labels = lax.broadcasted_iota(jnp.int32, (1, count), 1)
        stored = jnp.sum(
            jnp.where(tenant == labels, adapter_storage_rows[None, :], 0), axis=1, keepdims=True
        )
        place = lax.broadcasted_iota(jnp.int32, (1, count * rank), 1) // rank
        row_of = lax.rem(zi - place // own + n_adapter, n_adapter) * own + lax.rem(place, own)
        mask = stored == row_of

        def fold(values):
            values = jnp.where(mask, values, 0.0)
            return sum(values[:, a * rank : (a + 1) * rank] for a in range(count))

        def spread(low):
            return jnp.where(mask, jnp.tile(low, (1, count)), jnp.zeros((), low.dtype))

        def last(a, b):
            return lax.dot_general(a, b, (((1,), (1,)), ((), ())), preferred_element_type=f32)

        down_all, _, _ = chain_gather(down_own, n_adapter, zi)
        up_all, _, _ = chain_gather(up_own, n_adapter, zi)

        partial = jnp.dot(
            tokens, frozen_projection_weight, preferred_element_type=f32
        ).astype(half)
        base_out = tensor_scatter(partial, n_tensor, ti)
        dy_full = tensor_gather(output_gradient, n_tensor, ti)

        def blocks(terms):
            return list(terms.reshape(n_adapter, own * rank, width))

        low = tensor_sum(fold(last(tokens, down_all)), n_tensor)
        low = spread((adapter_scale * low).astype(half))
        terms_up = lax.dot_general(
            low, output_gradient, (((0,), (0,)), ((), ())), preferred_element_type=f32
        )
        grad_up = chain_scatter(blocks(terms_up), n_adapter)

        back_low = tensor_sum(fold(last(output_gradient, up_all)), n_tensor)
        back_low = spread((adapter_scale * back_low).astype(half))
        terms_down = lax.dot_general(
            back_low, tokens, (((0,), (0,)), ((), ())), preferred_element_type=f32
        )
        grad_down = chain_scatter(blocks(terms_down), n_adapter)

        delta = jnp.dot(low, up_all, preferred_element_type=f32).astype(half)
        back = jnp.dot(back_low, down_all, preferred_element_type=f32).astype(half)
        layer_result = (base_out + delta.astype(f32)).astype(half)
        base_back = last(dy_full, frozen_projection_weight)
        input_sensitivity = (base_back + back.astype(f32)).astype(half)

        shape = shrink_factor_matrices.shape
        p_up, m_up, v_up = optimizer_advance(
            expand_factor_matrices,
            grad_up.reshape(shape),
            expand_running_mean,
            expand_running_variance,
        )
        p_down, m_down, v_down = optimizer_advance(
            shrink_factor_matrices,
            grad_down.reshape(shape),
            shrink_running_mean,
            shrink_running_variance,
        )
        return (layer_result, input_sensitivity, p_down, p_up, m_down, m_up, v_down, v_up)

    return on_device


def solution(mesh):
    rows = P(("groups", "adapter"), "tensor")
    maps = P(("groups", "adapter"), None, "tensor")
    return jax.shard_map(
        make(mesh.shape["tensor"], mesh.shape["adapter"]),
        mesh=mesh,
        in_specs=(rows, P(("groups", "adapter"), None), P("groups"), P("tensor", None))
        + (maps,) * 6
        + (rows,),
        out_specs=(rows, rows) + (maps,) * 6,
        check_vma=False,
    )
```

time: 355 us -> 288 us (0.81)
  waiting for transfers between devices: 252 us -> 119 us
  starting transfers between devices: 0.47 us -> 64.2 us
  matrix products: 71.9 us -> 42.7 us
  local copies, waits for them, and re-layouts: 1.88 us -> 27.4 us
  other arithmetic: 12.3 us -> 29.3 us
  between operations: 14.2 us -> 1.28 us
    reduce_scatter x3 -> x0, waiting for transfers between devices: 136 us -> none  [the longest x1 71.6 us: on_device(): lax.psum_scatter(partial_value, 'tensor', scatter_dimension=1, tiled=True)]
    ppermute x0 -> x34, waiting for transfers between devices: none -> 119 us  [the longest x6 44.1 us: chain_scatter(): lax.ppermute(rightward.astype(half), 'adapter', [(i, i + 1) for i in rang...]
    all_gather x3 -> x0, waiting for transfers between devices: 83.2 us -> none  [the longest x1 42.3 us: on_device(): lax.all_gather(up_maps_half, 'adapter', axis=0, tiled=True)]
    ppermute x0 -> x34, starting transfers between devices: none -> 64.2 us  [the longest x6 15.1 us: chain_gather(): lax.ppermute(left[-1], 'adapter', [(i, i + 1) for i in range(t - 1, size...]
    psum x1 -> x0, waiting for transfers between devices: 31.5 us -> none  [on_device(): lax.psum((low_part, back_part), 'tensor')]
    dot_general x11 -> x7, matrix products: 53.4 us -> 26.3 us  [the longest x3 20.1 us: last(): lax.dot_general(a, b, (((1,), (1,)), ((), ())), preferred_element_type=f32)]
    dynamic_slice x0 -> x2, local copies, waits for them, and re-layouts: none -> 16.7 us  [the longest x1 13.1 us: tensor_scatter(): keep = lax.dynamic_index_in_dim(pairs, mine, 2, keepdims=False)]
    another operation x1 -> x3, local copies, waits for them, and re-layouts: 0.01 us -> 8.08 us  [the longest x1 7.82 us: tensor_scatter(): pairs = total.reshape(rows, -1, 2, width)]
  transfers between devices with their start and end apart: 7 -> 34, of which waited for: 7 -> 15; matrix products, arithmetic and copies ran while one was open for 21% -> 31% of each run, Pallas kernels for 0% -> 0%
where the time goes in v1:
time: 288 us; the launch traced here: 284 us
  waiting for transfers between devices  119 us (41%)
  starting transfers between devices  64.2 us (22%)
  matrix products  42.7 us (15%)
  other arithmetic  29.3 us (10%)
  local copies, waits for them, and re-layouts  27.4 us (10%)
    ppermute x6, waiting for transfers between devices, chain_scatter(): lax.ppermute(rightward.astype(half), 'adapter', [(i, i + 1) for i in rang...  44.1 us
    ppermute x6, waiting for transfers between devices, chain_gather(): lax.ppermute(right[-1], 'adapter', [(i, i - 1) for i in range(1, size - t...  32.1 us
    ppermute x6, waiting for transfers between devices, chain_scatter(): lax.ppermute(leftward.astype(half), 'adapter', [(i, i - 1) for i in range...  22.4 us
    dot_general x3, matrix products, last(): lax.dot_general(a, b, (((1,), (1,)), ((), ())), preferred_element_type=f32)  20.1 us
    dot_general x1, matrix products, on_device(): jnp.dot(tokens, frozen_projection_weight, preferred_element_type=f32)  16.3 us
    ppermute x6, waiting for transfers between devices, chain_gather(): lax.ppermute(left[-1], 'adapter', [(i, i + 1) for i in range(t - 1, size...  15.5 us
    ppermute x6, starting transfers between devices, chain_gather(): lax.ppermute(left[-1], 'adapter', [(i, i + 1) for i in range(t - 1, size...  15.1 us
    ppermute x6, starting transfers between devices, chain_scatter(): lax.ppermute(rightward.astype(half), 'adapter', [(i, i + 1) for i in rang...  14.7 us
  transfers between devices with their start and end apart: 34, of which 15 were waited for; matrix products, arithmetic and copies ran while one was open for 31% of the time, Pallas kernels for 0%

profile of v1, /device:TPU:15, one launch (start us, length us, event | category | flops | bytes accessed | tf_op | source)
XLA Modules:
  0.0 284.4 jit_solution(8520041894878695634)
XLA Ops:
  0.6 1.4 convert_element_type.142
  2.0 3.2 %collective-permute-start.2 = (bf16[128,2048]{1,0:T(8,128)(2,1)S(1)}, bf16[128,2048]{1,0:T(8,128)(2,1)S(1)}, u32[]{:S(2)}, u32[]{:S(2)}) collective-permute-start(bf16[128,2048]{1,0:T(8,128)(2,1)S(1)} %bitcast.63), channel_id=1, source_target_pairs={{0,1},{1,2},{2,3},{4,5},{5,6},{6,7},{8,9},{9,10},{10,11},{12,13},{... | collective-permute-start | bytes 1572872 | tf_op jit(solution)/shard_map/ppermute | solution.py:82
  5.3 2.1 collective-permute-start.3
  7.4 9.4 %collective-permute-done.2 = bf16[128,2048]{1,0:T(8,128)(2,1)S(1)} collective-permute-done((bf16[128,2048]{1,0:T(8,128)(2,1)S(1)}, bf16[128,2048]{1,0:T(8,128)(2,1)S(1)}, u32[]{:S(2)}, u32[]{:S(2)}) %collective-permute-start.2) | collective-permute-done | bytes 524320 | tf_op jit(solution)/shard_map/ppermute | solution.py:82
  16.7 4.0 %collective-permute-start.6 = (bf16[128,2048]{1,0:T(8,128)(2,1)S(1)}, bf16[128,2048]{1,0:T(8,128)(2,1)}, u32[]{:S(2)}, u32[]{:S(2)}) collective-permute-start(bf16[128,2048]{1,0:T(8,128)(2,1)S(1)} %collective-permute-done.2), channel_id=1, source_target_pairs={{1,2},{2,3},{5,6},{6,7},{9,10},{10,11},{13,14},{14,15},{17,18},{18... | collective-permute-start | bytes 1572872 | tf_op jit(solution)/shard_map/ppermute | solution.py:82
  20.7 1.9 collective-permute-start.4
  22.7 0.8 select_reduce_fusion
  23.4 6.1 %collective-permute-done.6 = bf16[128,2048]{1,0:T(8,128)(2,1)} collective-permute-done((bf16[128,2048]{1,0:T(8,128)(2,1)S(1)}, bf16[128,2048]{1,0:T(8,128)(2,1)}, u32[]{:S(2)}, u32[]{:S(2)}) %collective-permute-start.6) | collective-permute-done | bytes 524320 | tf_op jit(solution)/shard_map/ppermute | solution.py:82
  29.6 1.4 collective-permute-start.7
  31.1 3.3 %collective-permute-done.4 = bf16[128,2048]{1,0:T(8,128)(2,1)} collective-permute-done((bf16[128,2048]{1,0:T(8,128)(2,1)S(1)}, bf16[128,2048]{1,0:T(8,128)(2,1)}, u32[]{:S(2)}, u32[]{:S(2)}) %collective-permute-start.4) | collective-permute-done | bytes 524320 | tf_op jit(solution)/shard_map/ppermute | solution.py:85
  34.3 2.2 collective-permute-start.5
  36.5 1.1 broadcast_select_fusion.3
  37.8 7.8 %collective-permute-done.5 = bf16[128,2048]{1,0:T(8,128)(2,1)S(1)} collective-permute-done((bf16[128,2048]{1,0:T(8,128)(2,1)}, bf16[128,2048]{1,0:T(8,128)(2,1)S(1)}, u32[]{:S(2)}, u32[]{:S(2)}) %collective-permute-start.5) | collective-permute-done | bytes 524320 | tf_op jit(solution)/shard_map/ppermute | solution.py:85
  46.8 4.8 %collective-permute-start.10 = (f32[256,64]{0,1:T(8,128)S(1)}, f32[256,64]{0,1:T(8,128)S(1)}, u32[]{:S(2)}, u32[]{:S(2)}) collective-permute-start(f32[256,64]{0,1:T(8,128)S(1)} %slice_add_fusion.9), channel_id=1, source_target_pairs={{0,12},{4,8},{8,4},{12,0},{1,13},{5,9},{9,5},{13,1},{2,14},{6,10},... | collective-permute-start | bytes 196616 | tf_op jit(solution)/shard_map/ppermute | solution.py:28
  51.6 3.3 %collective-permute-done.10 = f32[256,64]{0,1:T(8,128)S(1)} collective-permute-done((f32[256,64]{0,1:T(8,128)S(1)}, f32[256,64]{0,1:T(8,128)S(1)}, u32[]{:S(2)}, u32[]{:S(2)}) %collective-permute-start.10) | collective-permute-done | bytes 65568 | tf_op jit(solution)/shard_map/ppermute | solution.py:28
  55.9 1.3 collective-permute-start.28
  57.9 13.5 %collective-permute-done.28 = bf16[128,2048]{1,0:T(8,128)(2,1)S(1)} collective-permute-done((bf16[128,2048]{1,0:T(8,128)(2,1)S(1)}, bf16[128,2048]{1,0:T(8,128)(2,1)S(1)}, u32[]{:S(2)}, u32[]{:S(2)}) %collective-permute-start.28) | collective-permute-done | bytes 524320 | tf_op jit(solution)/shard_map/ppermute | solution.py:98
  71.5 1.9 collective-permute-start.29
  73.5 12.7 %collective-permute-done.29 = bf16[128,2048]{1,0:T(8,128)(2,1)S(1)} collective-permute-done((bf16[128,2048]{1,0:T(8,128)(2,1)S(1)}, bf16[128,2048]{1,0:T(8,128)(2,1)S(1)}, u32[]{:S(2)}, u32[]{:S(2)}) %collective-permute-start.29) | collective-permute-done | bytes 524320 | tf_op jit(solution)/shard_map/ppermute | solution.py:98
  86.1 1.1 add_convert_fusion.2
  87.2 1.3 collective-permute-start.32
  88.5 4.0 %collective-permute-start.30 = (bf16[128,2048]{1,0:T(8,128)(2,1)}, bf16[128,2048]{1,0:T(8,128)(2,1)}, u32[]{:S(2)}, u32[]{:S(2)}) collective-permute-start(bf16[128,2048]{1,0:T(8,128)(2,1)} %get-tuple-element.14), channel_id=1, source_target_pairs={{0,1},{1,2},{2,3},{4,5},{5,6},{6,7},{8,9},{9,10},{10,11},{12,13},{... | collective-permute-start | bytes 1572872 | tf_op jit(solution)/shard_map/ppermute | solution.py:98
  92.5 8.5 %collective-permute-done.32 = bf16[128,2048]{1,0:T(8,128)(2,1)S(1)} collective-permute-done((bf16[128,2048]{1,0:T(8,128)(2,1)S(1)}, bf16[128,2048]{1,0:T(8,128)(2,1)S(1)}, u32[]{:S(2)}, u32[]{:S(2)}) %collective-permute-start.32) | collective-permute-done | bytes 524320 | tf_op jit(solution)/shard_map/ppermute | solution.py:101
  101.0 0.9 add_convert_fusion
  101.9 1.9 collective-permute-start.33
  104.4 10.6 %collective-permute-done.33 = bf16[128,2048]{1,0:T(8,128)(2,1)} collective-permute-done((bf16[128,2048]{1,0:T(8,128)(2,1)}, bf16[128,2048]{1,0:T(8,128)(2,1)}, u32[]{:S(2)}, u32[]{:S(2)}) %collective-permute-start.33) | collective-permute-done | bytes 524320 | tf_op jit(solution)/shard_map/ppermute | solution.py:101
  115.1 1.7 fusion.9
  116.8 4.5 %divide_subtract_fusion = (f32[2,64,2048]{2,1,0:T(8,128)}, f32[2,64,2048]{2,1,0:T(8,128)}, f32[2,64,2048]{2,1,0:T(8,128)}, bf16[2,64,2048]{2,1,0:T(8,128)(2,1)}) fusion(f32[2,64,2048]{2,1,0:T(8,128)} %param.16, f32[2,64,2048]{2,1,0:T(8,128)S(1)} %bitcast.59, f32[2,64,2048]{2,1,0:T(8,128)} %param.18, f32[2,64,2048]{2,1,0:T(8,128)} %param.20), kind=kLoop, calls=%fused_computation.31 | loop fusion | flops 3407872 | bytes 7864320 | tf_op jit(solution)/shard_map/sub | solution.py:21
  121.3 2.9 %collective-permute-start.11 = (bf16[128,2048]{1,0:T(8,128)(2,1)}, bf16[128,2048]{1,0:T(8,128)(2,1)}, u32[]{:S(2)}, u32[]{:S(2)}) collective-permute-start(bf16[128,2048]{1,0:T(8,128)(2,1)} %bitcast.7), channel_id=1, source_target_pairs={{0,1},{1,2},{2,3},{4,5},{5,6},{6,7},{8,9},{9,10},{10,11},{12,13},{... | collective-permute-start | bytes 1572872 | tf_op jit(solution)/shard_map/ppermute | solution.py:82
  124.1 16.3 %convolution_convert_fusion = bf16[256,8192]{1,0:T(8,128)(2,1)} fusion(bf16[256,2048]{1,0:T(8,128)(2,1)S(1)} %copy-done, bf16[2048,8192]{1,0:T(8,128)(2,1)} %param.14), kind=kOutput, calls=%fused_computation | convolution fusion | flops 8592031744 | bytes 38797312 | tf_op jit(solution)/shard_map/dot_general | solution.py:151
  140.5 7.8 %reshape_reshape.6 = bf16[256,2,2,2048]{3,2,1,0:T(2,128)(2,1)} reshape(bf16[256,8192]{1,0:T(8,128)(2,1)} %convolution_convert_fusion) | data formatting | bytes 8388608 | tf_op jit(solution)/shard_map/reshape;reshape | solution.py:57
  148.3 3.2 %collective-permute-start.12 = (bf16[128,2048]{1,0:T(8,128)(2,1)}, bf16[128,2048]{1,0:T(8,128)(2,1)}, u32[]{:S(2)}, u32[]{:S(2)}) collective-permute-start(bf16[128,2048]{1,0:T(8,128)(2,1)} %bitcast.7), channel_id=1, source_target_pairs={{1,0},{2,1},{3,2},{5,4},{6,5},{7,6},{9,8},{10,9},{11,10},{13,12},{... | collective-permute-start | bytes 1572872 | tf_op jit(solution)/shard_map/ppermute | solution.py:85
  151.5 2.9 %collective-permute-start.15 = (bf16[128,2048]{1,0:T(8,128)(2,1)}, bf16[128,2048]{1,0:T(8,128)(2,1)}, u32[]{:S(2)}, u32[]{:S(2)}) collective-permute-start(bf16[128,2048]{1,0:T(8,128)(2,1)} %collective-permute-done.11), channel_id=1, source_target_pairs={{1,2},{2,3},{5,6},{6,7},{9,10},{10,11},{13,14},{14,15},{17,18},{18... | collective-permute-start | bytes 1572872 | tf_op jit(solution)/shard_map/ppermute | solution.py:82
  154.4 13.1 %constant_dynamic-slice_fusion.1 = (bf16[256,2,1,2048]{3,2,1,0:T(2,128)(2,1)}, bf16[256,2,1,2048]{3,2,1,0:T(2,128)(2,1)S(1)}) fusion(bf16[256,2,2,2048]{3,2,1,0:T(2,128)(2,1)} %reshape_reshape.6, s32[]{:T(128)S(6)} %select_n.108, s32[]{:T(128)S(6)} %select_n.109), kind=kLoop, calls=%fused_computation.98 | loop fusion | bytes 8388616 | tf_op jit(solution)/shard_map/jit(dynamic_index_in_dim)/dynamic_slice | solution.py:59
  167.5 3.6 %copy.34 = bf16[256,2,1,2048]{3,0,1,2:T(8,128)(2,1)} copy(bf16[256,2,1,2048]{3,2,1,0:T(2,128)(2,1)S(1)} %get-tuple-element.25) | data formatting | bytes 4194304 | tf_op jit(solution)/shard_map/jit(dynamic_index_in_dim)/dynamic_slice | solution.py:60
  171.1 3.9 %collective-permute-start = (bf16[256,2,2048]{2,0,1:T(8,128)(2,1)}, bf16[256,2,2048]{2,0,1:T(8,128)(2,1)}, u32[]{:S(2)}, u32[]{:S(2)}) collective-permute-start(bf16[256,2,2048]{2,0,1:T(8,128)(2,1)} %bitcast.58), channel_id=1, source_target_pairs={{0,4},{4,0},{8,12},{12,8},{1,5},{5,1},{9,13},{13,9},{2,6},{6,2},{1... | collective-permute-start | bytes 6291464 | tf_op jit(solution)/shard_map/ppermute | solution.py:28
  175.0 1.9 collective-permute-start.13
  177.7 1.4 select_bitcast_fusion.3
  179.0 11.6 %collective-permute-done.13 = bf16[128,2048]{1,0:T(8,128)(2,1)S(1)} collective-permute-done((bf16[128,2048]{1,0:T(8,128)(2,1)}, bf16[128,2048]{1,0:T(8,128)(2,1)S(1)}, u32[]{:S(2)}, u32[]{:S(2)}) %collective-permute-start.13) | collective-permute-done | bytes 524320 | tf_op jit(solution)/shard_map/ppermute | solution.py:85
  190.7 2.1 collective-permute-start.14
  192.9 1.1 broadcast_select_fusion
  194.0 9.4 %collective-permute-done.14 = bf16[128,2048]{1,0:T(8,128)(2,1)S(1)} collective-permute-done((bf16[128,2048]{1,0:T(8,128)(2,1)S(1)}, bf16[128,2048]{1,0:T(8,128)(2,1)S(1)}, u32[]{:S(2)}, u32[]{:S(2)}) %collective-permute-start.14) | collective-permute-done | bytes 524320 | tf_op jit(solution)/shard_map/ppermute | solution.py:85
  203.5 1.1 broadcast_select_fusion.4
  204.6 1.8 fusion.5
  206.5 3.1 %collective-permute-start.21 = (f32[256,64]{0,1:T(8,128)S(1)}, f32[256,64]{0,1:T(8,128)S(1)}, u32[]{:S(2)}, u32[]{:S(2)}) collective-permute-start(f32[256,64]{0,1:T(8,128)S(1)} %slice_add_fusion.2), channel_id=1, source_target_pairs={{0,12},{4,8},{8,4},{12,0},{1,13},{5,9},{9,5},{13,1},{2,14},{6,10},... | collective-permute-start | bytes 196616 | tf_op jit(solution)/shard_map/ppermute | solution.py:28
  210.3 2.1 collective-permute-done.21
  213.5 1.6 collective-permute-start.22
  215.1 1.0 copy-done.4
  216.1 4.2 %convert_add_fusion = f32[256,2,2048]{2,0,1:T(8,128)S(1)} fusion(bf16[256,2,2048]{2,0,1:T(8,128)(2,1)} %collective-permute-done, bf16[256,2,1,2048]{3,2,1,0:T(2,128)(2,1)S(1)} %copy-done.4), kind=kLoop, calls=%fused_computation.2 | loop fusion | flops 3145728 | bytes 8388608 | tf_op jit(solution)/shard_map/add | solution.py:62
  221.2 8.0 %collective-permute-done.22 = bf16[128,2048]{1,0:T(8,128)(2,1)S(1)} collective-permute-done((bf16[128,2048]{1,0:T(8,128)(2,1)S(1)}, bf16[128,2048]{1,0:T(8,128)(2,1)S(1)}, u32[]{:S(2)}, u32[]{:S(2)}) %collective-permute-start.22) | collective-permute-done | bytes 524320 | tf_op jit(solution)/shard_map/ppermute | solution.py:98
  229.3 1.9 collective-permute-start.23
  231.6 2.4 pad_maximum_fusion
  233.9 10.0 %collective-permute-done.23 = bf16[128,2048]{1,0:T(8,128)(2,1)S(1)} collective-permute-done((bf16[128,2048]{1,0:T(8,128)(2,1)S(1)}, bf16[128,2048]{1,0:T(8,128)(2,1)S(1)}, u32[]{:S(2)}, u32[]{:S(2)}) %collective-permute-start.23) | collective-permute-done | bytes 524320 | tf_op jit(solution)/shard_map/ppermute | solution.py:98
  243.9 1.1 add_convert_fusion.6
  245.0 1.6 collective-permute-start.26
  246.7 2.8 fusion.3
  249.5 2.0 fusion.4
  251.5 4.0 %collective-permute-start.24 = (bf16[128,2048]{1,0:T(8,128)(2,1)}, bf16[128,2048]{1,0:T(8,128)(2,1)S(1)}, u32[]{:S(2)}, u32[]{:S(2)}) collective-permute-start(bf16[128,2048]{1,0:T(8,128)(2,1)} %get-tuple-element.18), channel_id=1, source_target_pairs={{0,1},{1,2},{2,3},{4,5},{5,6},{6,7},{8,9},{9,10},{10,11},{12,13},{... | collective-permute-start | bytes 1572872 | tf_op jit(solution)/shard_map/ppermute | solution.py:98
  255.5 3.3 %collective-permute-done.26 = bf16[128,2048]{1,0:T(8,128)(2,1)S(1)} collective-permute-done((bf16[128,2048]{1,0:T(8,128)(2,1)S(1)}, bf16[128,2048]{1,0:T(8,128)(2,1)S(1)}, u32[]{:S(2)}, u32[]{:S(2)}) %collective-permute-start.26) | collective-permute-done | bytes 524320 | tf_op jit(solution)/shard_map/ppermute | solution.py:101
  258.9 1.9 collective-permute-start.27
  260.8 17.6 %fusion = bf16[256,2048]{1,0:T(8,128)(2,1)} fusion(f32[256,2048]{1,0:T(8,128)} %fusion.4, bf16[256,8192]{0,1:T(8,128)(2,1)} %bitcast.62, bf16[2048,8192]{1,0:T(8,128)(2,1)} %param.14), kind=kOutput, calls=%fused_computation.4 | convolution fusion | flops 8590983168 | bytes 40894464 | tf_op jit(solution)/shard_map/dot_general | solution.py:146
  278.4 0.8 copy-done.16
  279.2 1.8 fusion.10
  281.0 3.3 %divide_subtract_fusion.1 = (f32[2,64,2048]{2,1,0:T(8,128)}, f32[2,64,2048]{2,1,0:T(8,128)}, f32[2,64,2048]{2,1,0:T(8,128)}) fusion(f32[2,64,2048]{2,1,0:T(8,128)S(1)} %copy-done.5, f32[2,64,2048]{2,1,0:T(8,128)S(1)} %bitcast.60, f32[2,64,2048]{2,1,0:T(8,128)S(1)} %copy-done.7, f32[2,64,2048]{2,1,0:T(8,128)} %param.19), kind=kLoop, calls=%fused_computation.37 | loop fusion | flops 3145728 | bytes 7340032 | tf_op jit(solution)/shard_map/sub | solution.py:21
  (83 shorter events, 7.9 us)
Async XLA Ops:
  0.6 45.0 %copy-start = (bf16[256,2048]{1,0:T(8,128)(2,1)S(1)}, bf16[256,2048]{1,0:T(8,128)(2,1)}, u32[]{:S(2)}) copy-start(bf16[256,2048]{1,0:T(8,128)(2,1)} %param.11) | copy-start | bytes 3145732
  2.0 44.4 %copy-start.8 = (bf16[2,64,2048]{2,1,0:T(8,128)(2,1)}, bf16[2,64,2048]{2,1,0:T(8,128)(2,1)S(1)}, u32[]{:S(2)}) copy-start(bf16[2,64,2048]{2,1,0:T(8,128)(2,1)S(1)} %convert_element_type.142) | copy-start | bytes 1572868
  2.0 14.7 %collective-permute-start.2 = (bf16[128,2048]{1,0:T(8,128)(2,1)S(1)}, bf16[128,2048]{1,0:T(8,128)(2,1)S(1)}, u32[]{:S(2)}, u32[]{:S(2)}) collective-permute-start(bf16[128,2048]{1,0:T(8,128)(2,1)S(1)} %bitcast.63), channel_id=1, source_target_pairs={{0,1},{1,2},{2,3},{4,5},{5,6},{6,7},{8,9},{9,10},{10,11},{12,13},{... | collective-permute-start | bytes 1572872 | tf_op jit(solution)/shard_map/ppermute | solution.py:82
  5.3 15.5 %collective-permute-start.3 = (bf16[128,2048]{1,0:T(8,128)(2,1)S(1)}, bf16[128,2048]{1,0:T(8,128)(2,1)S(1)}, u32[]{:S(2)}, u32[]{:S(2)}) collective-permute-start(bf16[128,2048]{1,0:T(8,128)(2,1)S(1)} %bitcast.64), channel_id=1, source_target_pairs={{1,0},{2,1},{3,2},{5,4},{6,5},{7,6},{9,8},{10,9},{11,10},{13,12},{... | collective-permute-start | bytes 1572872 | tf_op jit(solution)/shard_map/ppermute | solution.py:85
  16.7 12.8 %collective-permute-start.6 = (bf16[128,2048]{1,0:T(8,128)(2,1)S(1)}, bf16[128,2048]{1,0:T(8,128)(2,1)}, u32[]{:S(2)}, u32[]{:S(2)}) collective-permute-start(bf16[128,2048]{1,0:T(8,128)(2,1)S(1)} %collective-permute-done.2), channel_id=1, source_target_pairs={{1,2},{2,3},{5,6},{6,7},{9,10},{10,11},{13,14},{14,15},{17,18},{18... | collective-permute-start | bytes 1572872 | tf_op jit(solution)/shard_map/ppermute | solution.py:82
  20.7 13.6 %collective-permute-start.4 = (bf16[128,2048]{1,0:T(8,128)(2,1)S(1)}, bf16[128,2048]{1,0:T(8,128)(2,1)}, u32[]{:S(2)}, u32[]{:S(2)}) collective-permute-start(bf16[128,2048]{1,0:T(8,128)(2,1)S(1)} %collective-permute-done.3), channel_id=1, source_target_pairs={{1,0},{2,1},{5,4},{6,5},{9,8},{10,9},{13,12},{14,13},{17,16},{18,1... | collective-permute-start | bytes 1572872 | tf_op jit(solution)/shard_map/ppermute | solution.py:85
  29.6 8.1 %collective-permute-start.7 = (bf16[128,2048]{1,0:T(8,128)(2,1)}, bf16[128,2048]{1,0:T(8,128)(2,1)}, u32[]{:S(2)}, u32[]{:S(2)}) collective-permute-start(bf16[128,2048]{1,0:T(8,128)(2,1)} %collective-permute-done.6), channel_id=1, source_target_pairs={{2,3},{6,7},{10,11},{14,15},{18,19},{22,23},{26,27},{30,31}} | collective-permute-start | bytes 1572872 | tf_op jit(solution)/shard_map/ppermute | solution.py:82
  34.3 11.2 %collective-permute-start.5 = (bf16[128,2048]{1,0:T(8,128)(2,1)}, bf16[128,2048]{1,0:T(8,128)(2,1)S(1)}, u32[]{:S(2)}, u32[]{:S(2)}) collective-permute-start(bf16[128,2048]{1,0:T(8,128)(2,1)} %collective-permute-done.4), channel_id=1, source_target_pairs={{1,0},{5,4},{9,8},{13,12},{17,16},{21,20},{25,24},{29,28}} | collective-permute-start | bytes 1572872 | tf_op jit(solution)/shard_map/ppermute | solution.py:85
  37.7 8.7 %copy-start.10 = (bf16[128,2048]{1,0:T(8,128)(2,1)}, bf16[128,2048]{1,0:T(8,128)(2,1)S(1)}, u32[]{:S(2)}) copy-start(bf16[128,2048]{1,0:T(8,128)(2,1)S(1)} %broadcast_select_fusion.3) | copy-start | bytes 1572868
  37.8 8.7 %copy-start.12 = (bf16[128,2048]{1,0:T(8,128)(2,1)}, bf16[128,2048]{1,0:T(8,128)(2,1)S(1)}, u32[]{:S(2)}) copy-start(bf16[128,2048]{1,0:T(8,128)(2,1)S(1)} %broadcast_select_fusion.1) | copy-start | bytes 1572868
  45.6 0.8 copy-start.14
  45.6 9.4 %copy-start.6 = (bf16[256,2048]{1,0:T(8,128)(2,1)S(1)}, bf16[256,2048]{1,0:T(8,128)(2,1)}, u32[]{:S(2)}) copy-start(bf16[256,2048]{1,0:T(8,128)(2,1)} %param.21) | copy-start | bytes 3145732
  46.5 5.1 %collective-permute-start.9 = (f32[256,64]{0,1:T(8,128)S(1)}, f32[256,64]{0,1:T(8,128)S(1)}, u32[]{:S(2)}, u32[]{:S(2)}) collective-permute-start(f32[256,64]{0,1:T(8,128)S(1)} %slice_add_fusion.9), channel_id=1, source_target_pairs={{0,8},{4,12},{8,0},{12,4},{1,9},{5,13},{9,1},{13,5},{2,10},{6,14},... | collective-permute-start | bytes 196616 | tf_op jit(solution)/shard_map/ppermute | solution.py:28
  46.8 8.1 %collective-permute-start.10 = (f32[256,64]{0,1:T(8,128)S(1)}, f32[256,64]{0,1:T(8,128)S(1)}, u32[]{:S(2)}, u32[]{:S(2)}) collective-permute-start(f32[256,64]{0,1:T(8,128)S(1)} %slice_add_fusion.9), channel_id=1, source_target_pairs={{0,12},{4,8},{8,4},{12,0},{1,13},{5,9},{9,5},{13,1},{2,14},{6,10},... | collective-permute-start | bytes 196616 | tf_op jit(solution)/shard_map/ppermute | solution.py:28
  51.6 3.3 %collective-permute-start.8 = (f32[256,64]{0,1:T(8,128)S(1)}, f32[256,64]{0,1:T(8,128)S(1)}, u32[]{:S(2)}, u32[]{:S(2)}) collective-permute-start(f32[256,64]{0,1:T(8,128)S(1)} %slice_add_fusion.9), channel_id=1, source_target_pairs={{0,4},{4,0},{8,12},{12,8},{1,5},{5,1},{9,13},{13,9},{2,6},{6,2},{1... | collective-permute-start | bytes 196616 | tf_op jit(solution)/shard_map/ppermute | solution.py:28
  55.8 45.2 %copy-start.3 = (f32[512,2048]{1,0:T(8,128)}, f32[512,2048]{1,0:T(8,128)S(1)}, u32[]{:S(2)}) copy-start(f32[512,2048]{1,0:T(8,128)S(1)} %fusion.31) | copy-start | bytes 12582916
  55.9 15.5 %collective-permute-start.28 = (bf16[128,2048]{1,0:T(8,128)(2,1)S(1)}, bf16[128,2048]{1,0:T(8,128)(2,1)S(1)}, u32[]{:S(2)}, u32[]{:S(2)}) collective-permute-start(bf16[128,2048]{1,0:T(8,128)(2,1)S(1)} %get-tuple-element.16), channel_id=1, source_target_pairs={{0,1},{4,5},{8,9},{12,13},{16,17},{20,21},{24,25},{28,29}} | collective-permute-start | bytes 1572872 | tf_op jit(solution)/shard_map/ppermute | solution.py:98
  57.2 16.2 %collective-permute-start.31 = (bf16[128,2048]{1,0:T(8,128)(2,1)S(1)}, bf16[128,2048]{1,0:T(8,128)(2,1)S(1)}, u32[]{:S(2)}, u32[]{:S(2)}) collective-permute-start(bf16[128,2048]{1,0:T(8,128)(2,1)S(1)} %get-tuple-element.17), channel_id=1, source_target_pairs={{3,2},{7,6},{11,10},{15,14},{19,18},{23,22},{27,26},{31,30}} | collective-permute-start | bytes 1572872 | tf_op jit(solution)/shard_map/ppermute | solution.py:101
  71.5 14.6 %collective-permute-start.29 = (bf16[128,2048]{1,0:T(8,128)(2,1)S(1)}, bf16[128,2048]{1,0:T(8,128)(2,1)S(1)}, u32[]{:S(2)}, u32[]{:S(2)}) collective-permute-start(bf16[128,2048]{1,0:T(8,128)(2,1)S(1)} %add_convert_fusion.3), channel_id=1, source_target_pairs={{0,1},{1,2},{4,5},{5,6},{8,9},{9,10},{12,13},{13,14},{16,17},{17,1... | collective-permute-start | bytes 1572872 | tf_op jit(solution)/shard_map/ppermute | solution.py:98
  87.2 13.8 %collective-permute-start.32 = (bf16[128,2048]{1,0:T(8,128)(2,1)S(1)}, bf16[128,2048]{1,0:T(8,128)(2,1)S(1)}, u32[]{:S(2)}, u32[]{:S(2)}) collective-permute-start(bf16[128,2048]{1,0:T(8,128)(2,1)S(1)} %get-tuple-element.15), channel_id=1, source_target_pairs={{2,1},{3,2},{6,5},{7,6},{10,9},{11,10},{14,13},{15,14},{18,17},{19... | collective-permute-start | bytes 1572872 | tf_op jit(solution)/shard_map/ppermute | solution.py:101
  88.5 15.9 %collective-permute-start.30 = (bf16[128,2048]{1,0:T(8,128)(2,1)}, bf16[128,2048]{1,0:T(8,128)(2,1)}, u32[]{:S(2)}, u32[]{:S(2)}) collective-permute-start(bf16[128,2048]{1,0:T(8,128)(2,1)} %get-tuple-element.14), channel_id=1, source_target_pairs={{0,1},{1,2},{2,3},{4,5},{5,6},{6,7},{8,9},{9,10},{10,11},{12,13},{... | collective-permute-start | bytes 1572872 | tf_op jit(solution)/shard_map/ppermute | solution.py:98
  101.9 13.2 %collective-permute-start.33 = (bf16[128,2048]{1,0:T(8,128)(2,1)}, bf16[128,2048]{1,0:T(8,128)(2,1)}, u32[]{:S(2)}, u32[]{:S(2)}) collective-permute-start(bf16[128,2048]{1,0:T(8,128)(2,1)} %add_convert_fusion), channel_id=1, source_target_pairs={{1,0},{2,1},{3,2},{5,4},{6,5},{7,6},{9,8},{10,9},{11,10},{13,12},{... | collective-permute-start | bytes 1572872 | tf_op jit(solution)/shard_map/ppermute | solution.py:101
  104.3 73.3 %collective-permute-start.17 = (bf16[256,1,2048]{0,2,1:T(8,128)(2,1)S(1)}, bf16[256,1,2048]{0,2,1:T(8,128)(2,1)}, u32[]{:S(2)}, u32[]{:S(2)}) collective-permute-start(bf16[256,1,2048]{0,2,1:T(8,128)(2,1)S(1)} %bitcast.61), channel_id=1, source_target_pairs={{0,8},{4,12},{8,0},{12,4},{1,9},{5,13},{9,1},{13,5},{2,10},{6,14},... | collective-permute-start | bytes 3145736 | tf_op jit(solution)/shard_map/ppermute | solution.py:28
  121.3 30.2 %collective-permute-start.11 = (bf16[128,2048]{1,0:T(8,128)(2,1)}, bf16[128,2048]{1,0:T(8,128)(2,1)}, u32[]{:S(2)}, u32[]{:S(2)}) collective-permute-start(bf16[128,2048]{1,0:T(8,128)(2,1)} %bitcast.7), channel_id=1, source_target_pairs={{0,1},{1,2},{2,3},{4,5},{5,6},{6,7},{8,9},{9,10},{10,11},{12,13},{... | collective-permute-start | bytes 1572872 | tf_op jit(solution)/shard_map/ppermute | solution.py:82
  148.3 26.7 %collective-permute-start.12 = (bf16[128,2048]{1,0:T(8,128)(2,1)}, bf16[128,2048]{1,0:T(8,128)(2,1)}, u32[]{:S(2)}, u32[]{:S(2)}) collective-permute-start(bf16[128,2048]{1,0:T(8,128)(2,1)} %bitcast.7), channel_id=1, source_target_pairs={{1,0},{2,1},{3,2},{5,4},{6,5},{7,6},{9,8},{10,9},{11,10},{13,12},{... | collective-permute-start | bytes 1572872 | tf_op jit(solution)/shard_map/ppermute | solution.py:85
  151.5 25.4 %collective-permute-start.15 = (bf16[128,2048]{1,0:T(8,128)(2,1)}, bf16[128,2048]{1,0:T(8,128)(2,1)}, u32[]{:S(2)}, u32[]{:S(2)}) collective-permute-start(bf16[128,2048]{1,0:T(8,128)(2,1)} %collective-permute-done.11), channel_id=1, source_target_pairs={{1,2},{2,3},{5,6},{6,7},{9,10},{10,11},{13,14},{14,15},{17,18},{18... | collective-permute-start | bytes 1572872 | tf_op jit(solution)/shard_map/ppermute | solution.py:82
  171.1 43.9 %collective-permute-start = (bf16[256,2,2048]{2,0,1:T(8,128)(2,1)}, bf16[256,2,2048]{2,0,1:T(8,128)(2,1)}, u32[]{:S(2)}, u32[]{:S(2)}) collective-permute-start(bf16[256,2,2048]{2,0,1:T(8,128)(2,1)} %bitcast.58), channel_id=1, source_target_pairs={{0,4},{4,0},{8,12},{12,8},{1,5},{5,1},{9,13},{13,9},{2,6},{6,2},{1... | collective-permute-start | bytes 6291464 | tf_op jit(solution)/shard_map/ppermute | solution.py:28
  175.0 15.6 %collective-permute-start.13 = (bf16[128,2048]{1,0:T(8,128)(2,1)}, bf16[128,2048]{1,0:T(8,128)(2,1)S(1)}, u32[]{:S(2)}, u32[]{:S(2)}) collective-permute-start(bf16[128,2048]{1,0:T(8,128)(2,1)} %collective-permute-done.12), channel_id=1, source_target_pairs={{1,0},{2,1},{5,4},{6,5},{9,8},{10,9},{13,12},{14,13},{17,16},{18,1... | collective-permute-start | bytes 1572872 | tf_op jit(solution)/shard_map/ppermute | solution.py:85
  176.9 16.0 %collective-permute-start.16 = (bf16[128,2048]{1,0:T(8,128)(2,1)}, bf16[128,2048]{1,0:T(8,128)(2,1)S(1)}, u32[]{:S(2)}, u32[]{:S(2)}) collective-permute-start(bf16[128,2048]{1,0:T(8,128)(2,1)} %collective-permute-done.15), channel_id=1, source_target_pairs={{2,3},{6,7},{10,11},{14,15},{18,19},{22,23},{26,27},{30,31}} | collective-permute-start | bytes 1572872 | tf_op jit(solution)/shard_map/ppermute | solution.py:82
  190.7 12.8 %collective-permute-start.14 = (bf16[128,2048]{1,0:T(8,128)(2,1)S(1)}, bf16[128,2048]{1,0:T(8,128)(2,1)S(1)}, u32[]{:S(2)}, u32[]{:S(2)}) collective-permute-start(bf16[128,2048]{1,0:T(8,128)(2,1)S(1)} %collective-permute-done.13), channel_id=1, source_target_pairs={{1,0},{5,4},{9,8},{13,12},{17,16},{21,20},{25,24},{29,28}} | collective-permute-start | bytes 1572872 | tf_op jit(solution)/shard_map/ppermute | solution.py:85
  206.4 3.9 %collective-permute-start.20 = (f32[256,64]{0,1:T(8,128)S(1)}, f32[256,64]{0,1:T(8,128)S(1)}, u32[]{:S(2)}, u32[]{:S(2)}) collective-permute-start(f32[256,64]{0,1:T(8,128)S(1)} %slice_add_fusion.2), channel_id=1, source_target_pairs={{0,8},{4,12},{8,0},{12,4},{1,9},{5,13},{9,1},{13,5},{2,10},{6,14},... | collective-permute-start | bytes 196616 | tf_op jit(solution)/shard_map/ppermute | solution.py:28
  206.5 5.9 %collective-permute-start.21 = (f32[256,64]{0,1:T(8,128)S(1)}, f32[256,64]{0,1:T(8,128)S(1)}, u32[]{:S(2)}, u32[]{:S(2)}) collective-permute-start(f32[256,64]{0,1:T(8,128)S(1)} %slice_add_fusion.2), channel_id=1, source_target_pairs={{0,12},{4,8},{8,4},{12,0},{1,13},{5,9},{9,5},{13,1},{2,14},{6,10},... | collective-permute-start | bytes 196616 | tf_op jit(solution)/shard_map/ppermute | solution.py:28
  209.6 2.9 %collective-permute-start.19 = (f32[256,64]{0,1:T(8,128)S(1)}, f32[256,64]{0,1:T(8,128)S(1)}, u32[]{:S(2)}, u32[]{:S(2)}) collective-permute-start(f32[256,64]{0,1:T(8,128)S(1)} %slice_add_fusion.2), channel_id=1, source_target_pairs={{0,4},{4,0},{8,12},{12,8},{1,5},{5,1},{9,13},{13,9},{2,6},{6,2},{1... | collective-permute-start | bytes 196616 | tf_op jit(solution)/shard_map/ppermute | solution.py:28
  209.8 21.5 %collective-permute-start.18 = (bf16[256,2,2048]{0,2,1:T(8,128)(2,1)S(1)}, bf16[256,2,2048]{0,2,1:T(8,128)(2,1)S(1)}, u32[]{:S(2)}, u32[]{:S(2)}) collective-permute-start(bf16[256,2,2048]{0,2,1:T(8,128)(2,1)S(1)} %maximum_bitcast_fusion), channel_id=1, source_target_pairs={{0,4},{4,0},{8,12},{12,8},{1,5},{5,1},{9,13},{13,9},{2,6},{6,2},{1... | collective-permute-start | bytes 6291464 | tf_op jit(solution)/shard_map/ppermute | solution.py:28
  212.6 3.5 %copy-start.4 = (bf16[256,2,1,2048]{3,2,1,0:T(2,128)(2,1)S(1)}, bf16[256,2,1,2048]{3,2,1,0:T(2,128)(2,1)}, u32[]{:S(2)}) copy-start(bf16[256,2,1,2048]{3,2,1,0:T(2,128)(2,1)} %get-tuple-element.24) | copy-start | bytes 6291460
  213.3 45.4 %copy-start.2 = (f32[512,2048]{1,0:T(8,128)}, f32[512,2048]{1,0:T(8,128)S(1)}, u32[]{:S(2)}) copy-start(f32[512,2048]{1,0:T(8,128)S(1)} %fusion.30) | copy-start | bytes 12582916
  213.5 15.7 %collective-permute-start.22 = (bf16[128,2048]{1,0:T(8,128)(2,1)S(1)}, bf16[128,2048]{1,0:T(8,128)(2,1)S(1)}, u32[]{:S(2)}, u32[]{:S(2)}) collective-permute-start(bf16[128,2048]{1,0:T(8,128)(2,1)S(1)} %get-tuple-element.20), channel_id=1, source_target_pairs={{0,1},{4,5},{8,9},{12,13},{16,17},{20,21},{24,25},{28,29}} | collective-permute-start | bytes 1572872 | tf_op jit(solution)/shard_map/ppermute | solution.py:98
  220.4 26.2 %collective-permute-start.1 = (bf16[256,1,2048]{2,0,1:T(8,128)(2,1)S(1)}, bf16[256,1,2048]{2,0,1:T(8,128)(2,1)S(1)}, u32[]{:S(2)}, u32[]{:S(2)}) collective-permute-start(bf16[256,1,2048]{2,0,1:T(8,128)(2,1)S(1)} %dynamic-slice_convert_fusion), channel_id=1, source_target_pairs={{0,8},{4,12},{8,0},{12,4},{1,9},{5,13},{9,1},{13,5},{2,10},{6,14},... | collective-permute-start | bytes 3145736 | tf_op jit(solution)/shard_map/ppermute | solution.py:28
  220.5 13.4 %collective-permute-start.25 = (bf16[128,2048]{1,0:T(8,128)(2,1)S(1)}, bf16[128,2048]{1,0:T(8,128)(2,1)S(1)}, u32[]{:S(2)}, u32[]{:S(2)}) collective-permute-start(bf16[128,2048]{1,0:T(8,128)(2,1)S(1)} %get-tuple-element.21), channel_id=1, source_target_pairs={{3,2},{7,6},{11,10},{15,14},{19,18},{23,22},{27,26},{31,30}} | collective-permute-start | bytes 1572872 | tf_op jit(solution)/shard_map/ppermute | solution.py:101
  229.3 14.6 %collective-permute-start.23 = (bf16[128,2048]{1,0:T(8,128)(2,1)S(1)}, bf16[128,2048]{1,0:T(8,128)(2,1)S(1)}, u32[]{:S(2)}, u32[]{:S(2)}) collective-permute-start(bf16[128,2048]{1,0:T(8,128)(2,1)S(1)} %add_convert_fusion.7), channel_id=1, source_target_pairs={{0,1},{1,2},{4,5},{5,6},{8,9},{9,10},{12,13},{13,14},{16,17},{17,1... | collective-permute-start | bytes 1572872 | tf_op jit(solution)/shard_map/ppermute | solution.py:98
  245.0 4.5 %copy-start.9 = (bf16[2,64,2048]{2,1,0:T(8,128)(2,1)S(1)}, bf16[2,64,2048]{2,1,0:T(8,128)(2,1)}, u32[]{:S(2)}) copy-start(bf16[2,64,2048]{2,1,0:T(8,128)(2,1)} %copy-done.8) | copy-start | bytes 1572868
  245.0 4.5 %copy-start.11 = (bf16[128,2048]{1,0:T(8,128)(2,1)S(1)}, bf16[128,2048]{1,0:T(8,128)(2,1)}, u32[]{:S(2)}) copy-start(bf16[128,2048]{1,0:T(8,128)(2,1)} %copy-done.10) | copy-start | bytes 1572868
  245.0 4.5 %copy-start.13 = (bf16[128,2048]{1,0:T(8,128)(2,1)S(1)}, bf16[128,2048]{1,0:T(8,128)(2,1)}, u32[]{:S(2)}) copy-start(bf16[128,2048]{1,0:T(8,128)(2,1)} %copy-done.12) | copy-start | bytes 1572868
  245.0 4.5 %copy-start.15 = (bf16[128,2048]{1,0:T(8,128)(2,1)S(1)}, bf16[128,2048]{1,0:T(8,128)(2,1)}, u32[]{:S(2)}) copy-start(bf16[128,2048]{1,0:T(8,128)(2,1)} %copy-done.14) | copy-start | bytes 1572868
  245.0 13.8 %collective-permute-start.26 = (bf16[128,2048]{1,0:T(8,128)(2,1)S(1)}, bf16[128,2048]{1,0:T(8,128)(2,1)S(1)}, u32[]{:S(2)}, u32[]{:S(2)}) collective-permute-start(bf16[128,2048]{1,0:T(8,128)(2,1)S(1)} %get-tuple-element.19), channel_id=1, source_target_pairs={{2,1},{3,2},{6,5},{7,6},{10,9},{11,10},{14,13},{15,14},{18,17},{19... | collective-permute-start | bytes 1572872 | tf_op jit(solution)/shard_map/ppermute | solution.py:101
  251.5 26.9 %collective-permute-start.24 = (bf16[128,2048]{1,0:T(8,128)(2,1)}, bf16[128,2048]{1,0:T(8,128)(2,1)S(1)}, u32[]{:S(2)}, u32[]{:S(2)}) collective-permute-start(bf16[128,2048]{1,0:T(8,128)(2,1)} %get-tuple-element.18), channel_id=1, source_target_pairs={{0,1},{1,2},{2,3},{4,5},{5,6},{6,7},{8,9},{9,10},{10,11},{12,13},{... | collective-permute-start | bytes 1572872 | tf_op jit(solution)/shard_map/ppermute | solution.py:98
  258.9 20.3 %collective-permute-start.27 = (bf16[128,2048]{1,0:T(8,128)(2,1)S(1)}, bf16[128,2048]{1,0:T(8,128)(2,1)}, u32[]{:S(2)}, u32[]{:S(2)}) collective-permute-start(bf16[128,2048]{1,0:T(8,128)(2,1)S(1)} %add_convert_fusion.4), channel_id=1, source_target_pairs={{1,0},{2,1},{3,2},{5,4},{6,5},{7,6},{9,8},{10,9},{11,10},{13,12},{... | collective-permute-start | bytes 1572872 | tf_op jit(solution)/shard_map/ppermute | solution.py:101
  260.8 20.2 %copy-start.5 = (f32[2,64,2048]{2,1,0:T(8,128)S(1)}, f32[2,64,2048]{2,1,0:T(8,128)}, u32[]{:S(2)}) copy-start(f32[2,64,2048]{2,1,0:T(8,128)} %param.15) | copy-start | bytes 3145732
  260.8 20.2 %copy-start.7 = (f32[2,64,2048]{2,1,0:T(8,128)S(1)}, f32[2,64,2048]{2,1,0:T(8,128)}, u32[]{:S(2)}) copy-start(f32[2,64,2048]{2,1,0:T(8,128)} %param.17) | copy-start | bytes 3145732
  278.4 0.8 copy-start.16
  279.2 5.2 %copy-start.1 = (bf16[256,2048]{1,0:T(8,128)(2,1)S(1)}, bf16[256,2048]{1,0:T(8,128)(2,1)}, u32[]{:S(2)}) copy-start(bf16[256,2048]{1,0:T(8,128)(2,1)} %param.11) | copy-start | bytes 3145732

commit v2 on v1

--- a/solution.py
+++ b/solution.py
@@ -1,6 +1,8 @@
 import jax
 import jax.numpy as jnp
 from jax import lax
+from jax.experimental import pallas as pl
+from jax.experimental.pallas import tpu as pltpu
 from jax.sharding import PartitionSpec as P
 
 beta_one = 0.9
@@ -105,6 +107,343 @@
     if from_left is not None:
         total = total + from_left.astype(f32) + from_right.astype(f32)
     return total
+
+
+TILE = 512
+MESH = pl.DeviceIdType.MESH
+
+
+def dot_last(a, b):
+    return lax.dot_general(a, b, (((1,), (1,)), ((), ())), preferred_element_type=f32)
+
+
+def dot_first(a, b):
+    return lax.dot_general(a, b, (((0,), (0,)), ((), ())), preferred_element_type=f32)
+
+
+def fused_kernel(
+    x, dy, mask, down, up, w,
+    layer, sens, grad_down, grad_up,
+    g_down, g_up, t_down, t_up, r_down, r_up,
+    part, near, far, dyg, acc, lows, low_in, spread_low,
+    wbuf, w_sem, z_send, z_recv, r_send, r_recv, y_send, y_recv, l_send, l_recv,
+):
+    zi, ti = lax.axis_index("adapter"), lax.axis_index("tensor")
+    nz = 4
+    peers = [ti, ti + 1 - 2 * (ti % 2), (ti + 2) % 4, 3 - ti]
+    width = x.shape[1]
+    tiles = width // TILE
+
+    def when(cond, fn):
+        pl.when(cond)(fn)
+
+    barrier = pltpu.get_barrier_semaphore()
+    when(zi > 0, lambda: pl.semaphore_signal(
+        barrier, inc=1, device_id={"adapter": zi - 1}, device_id_type=MESH))
+    when(zi < nz - 1, lambda: pl.semaphore_signal(
+        barrier, inc=1, device_id={"adapter": zi + 1}, device_id_type=MESH))
+    for k in (1, 2, 3):
+        pl.semaphore_signal(barrier, inc=1, device_id={"tensor": peers[k]}, device_id_type=MESH)
+    g_down[zi] = down[...].astype(half)
+    g_up[zi] = up[...].astype(half)
+
+    order = [3, 2, 1, 0, 0, 1, 2, 3]
+
+    def w_copy(s, j, slot):
+        column = pl.multiple_of(peers[order[s]] * width + j * TILE, TILE)
+        return pltpu.make_async_copy(w.at[:, pl.ds(column, TILE)], wbuf.at[slot], w_sem.at[slot])
+
+    w_copy(0, 0, 0).start()
+    inside = (zi > 0) & (zi < nz - 1)
+    when(inside, lambda: pl.semaphore_wait(barrier, 5))
+    when(jnp.logical_not(inside), lambda: pl.semaphore_wait(barrier, 4))
+
+    def remote_z(src, dst, send, recv, direction):
+        to = zi + 1 if direction == 0 else zi - 1
+        return pltpu.make_async_remote_copy(
+            src_ref=src, dst_ref=dst, send_sem=send, recv_sem=recv,
+            device_id={"adapter": to}, device_id_type=MESH)
+
+    def gather_copy(kind, t, direction, owner):
+        g = (g_down, g_up)[kind]
+        return remote_z(g.at[owner], g.at[owner], z_send.at[kind, direction, t - 1],
+                        z_recv.at[kind, direction, t - 1], direction)
+
+    def may_right(t):
+        return (zi < nz - 1) & (zi - t + 1 >= 0)
+
+    def may_left(t):
+        return (zi > 0) & (zi + t - 1 <= nz - 1)
+
+    def hop(kind, t):
+        when(may_right(t), lambda: gather_copy(kind, t, 0, zi - t + 1).start())
+        when(may_left(t), lambda: gather_copy(kind, t, 1, zi + t - 1).start())
+
+    def land(kind, t):
+        when(zi - t >= 0, lambda: gather_copy(kind, t, 0, zi - t).wait_recv())
+        when(zi + t <= nz - 1, lambda: gather_copy(kind, t, 1, zi + t).wait_recv())
+
+    def sent(kind, t):
+        when(may_right(t), lambda: gather_copy(kind, t, 0, zi - t + 1).wait_send())
+        when(may_left(t), lambda: gather_copy(kind, t, 1, zi + t - 1).wait_send())
+
+    def reduce_copy(kind, d, direction, owner):
+        terms, arrived = ((t_down, r_down), (t_up, r_up))[kind]
+        return remote_z(terms.at[owner], arrived.at[direction, d - 1],
+                        r_send.at[kind, direction, d - 1], r_recv.at[kind, direction, d - 1],
+                        direction)
+
+    def reduce_hop(kind, d):
+        terms, arrived = ((t_down, r_down), (t_up, r_up))[kind]
+
+        def go(direction):
+            owner = zi + d if direction == 0 else zi - d
+
+            def fn():
+                if d < nz - 1:
+                    def add():
+                        terms[owner] = (
+                            terms[owner].astype(f32) + arrived[direction, d].astype(f32)
+                        ).astype(half)
+
+                    when(zi > 0 if direction == 0 else zi < nz - 1, add)
+                reduce_copy(kind, d, direction, owner).start()
+
+            return fn
+
+        when(zi + d <= nz - 1, go(0))
+        when(zi - d >= 0, go(1))
+
+    def reduce_land(kind, d):
+        when((zi > 0) & (zi - 1 + d <= nz - 1),
+             lambda: reduce_copy(kind, d, 0, 0).wait_recv())
+        when((zi < nz - 1) & (zi + 1 - d >= 0),
+             lambda: reduce_copy(kind, d, 1, 0).wait_recv())
+
+    def reduce_sent(kind, d):
+        when(zi + d <= nz - 1, lambda: reduce_copy(kind, d, 0, zi + d).wait_send())
+        when(zi - d >= 0, lambda: reduce_copy(kind, d, 1, zi - d).wait_send())
+
+    def reduce_end(kind, out):
+        terms, arrived = ((t_down, r_down), (t_up, r_up))[kind]
+        out[...] = terms[zi].astype(f32)
+
+        def add(direction):
+            def fn():
+                out[...] += arrived[direction, 0].astype(f32)
+            return fn
+
+        when(zi > 0, add(0))
+        when(zi < nz - 1, add(1))
+
+    def remote_y(src, dst, n, k):
+        return pltpu.make_async_remote_copy(
+            src_ref=src, dst_ref=dst, send_sem=y_send.at[n], recv_sem=y_recv.at[n],
+            device_id={"tensor": peers[k]}, device_id_type=MESH)
+
+    dy_far = remote_y(dy, dyg.at[1], 0, 2)
+    dy_near = remote_y(dy, dyg.at[0], 1, 1)
+    dy_relay = remote_y(dyg.at[1], dyg.at[2], 2, 1)
+    near_first = remote_y(part.at[3], near.at[0], 3, 1)
+    near_second = remote_y(part.at[1], near.at[1], 4, 1)
+    far_copy = remote_y(part.at[2], far, 5, 2)
+
+    def stream(s, use):
+        def step(j, carry):
+            slot = lax.rem(j, 2)
+            w_copy(s, j, slot).wait()
+
+            @pl.when(j < tiles - 1)
+            def _():
+                w_copy(s, j + 1, 1 - slot).start()
+
+            if s + 1 < len(order):
+                @pl.when(j == tiles - 1)
+                def _():
+                    w_copy(s + 1, 0, 1 - slot).start()
+
+            use(pl.ds(pl.multiple_of(j * TILE, TILE), TILE), wbuf.at[slot])
+            return carry
+
+        lax.fori_loop(0, tiles, step, 0)
+
+    def forward(s):
+        def use(columns, tile):
+            part[order[s], :, columns] = jnp.dot(
+                x[...], tile[...], preferred_element_type=f32
+            ).astype(half)
+        stream(s, use)
+
+    def backward(s):
+        k = order[s]
+        source = dy if k == 0 else dyg.at[k - 1]
+
+        def use(columns, tile):
+            acc[...] += dot_last(source[:, columns], tile[...])
+        stream(s, use)
+
+    def low_start(kind, tokens, maps):
+        total = jnp.zeros((x.shape[0], 128), f32)
+        for o in range(nz):
+            product = dot_last(tokens[...], maps[o])
+            total += jnp.where(mask[:, o * 128:(o + 1) * 128] > 0.5, product, 0.0)
+        lows[kind] = total
+        for k in (1, 2, 3):
+            low_copy(kind, k).start()
+
+    def low_copy(kind, k):
+        return pltpu.make_async_remote_copy(
+            src_ref=lows.at[kind], dst_ref=low_in.at[kind, k - 1],
+            send_sem=l_send.at[kind, k - 1], recv_sem=l_recv.at[kind, k - 1],
+            device_id={"tensor": peers[k]}, device_id_type=MESH)
+
+    def low_end(kind, tokens, terms):
+        for k in (1, 2, 3):
+            low_copy(kind, k).wait_recv()
+        total = (lows[kind] + low_in[kind, 0]) + (low_in[kind, 1] + low_in[kind, 2])
+        value = adapter_scale * total
+        for o in range(nz):
+            block = jnp.where(mask[:, o * 128:(o + 1) * 128] > 0.5, value, 0.0).astype(half)
+            spread_low[kind, :, o * 128:(o + 1) * 128] = block
+            terms[o] = dot_first(block, tokens[...]).astype(half)
+
+    def expand(kind, maps, columns):
+        total = jnp.zeros((x.shape[0], TILE), f32)
+        for o in range(nz):
+            total += jnp.dot(spread_low[kind, :, o * 128:(o + 1) * 128], maps[o, :, columns],
+                             preferred_element_type=f32)
+        return total.astype(half).astype(f32)
+
+    hop(0, 1)
+    dy_far.start()
+    dy_near.start()
+    acc[...] = jnp.zeros_like(acc)
+    forward(0)
+    near_first.start()
+    forward(1)
+    near_first.wait_recv()
+    part[2] = (part[2].astype(f32) + near[0].astype(f32)).astype(half)
+    far_copy.start()
+    land(0, 1)
+    hop(0, 2)
+    forward(2)
+    near_second.start()
+    forward(3)
+    land(0, 2)
+    hop(0, 3)
+    dy_far.wait_recv()
+    dy_relay.start()
+    backward(4)
+    land(0, 3)
+    hop(1, 1)
+    low_start(0, x, g_down)
+    dy_near.wait_recv()
+    low_end(0, dy, t_up)
+    reduce_hop(1, 3)
+    backward(5)
+    land(1, 1)
+    hop(1, 2)
+    reduce_land(1, 3)
+    reduce_hop(1, 2)
+    backward(6)
+    land(1, 2)
+    hop(1, 3)
+    reduce_land(1, 2)
+    reduce_hop(1, 1)
+    dy_relay.wait_recv()
+    backward(7)
+    land(1, 3)
+    low_start(1, dy, g_up)
+    low_end(1, x, t_down)
+    reduce_hop(0, 3)
+    reduce_land(1, 1)
+    reduce_end(1, grad_up)
+    near_second.wait_recv()
+    far_copy.wait_recv()
+
+    def finish_forward(j, carry):
+        columns = pl.ds(pl.multiple_of(j * TILE, TILE), TILE)
+        base = part[0, :, columns].astype(f32) + near[1, :, columns].astype(f32)
+        base = base + far[:, columns].astype(f32)
+        layer[:, columns] = (base + expand(0, g_up, columns)).astype(half)
+        return carry
+
+    def finish_backward(j, carry):
+        columns = pl.ds(pl.multiple_of(j * TILE, TILE), TILE)
+        sens[:, columns] = (acc[:, columns] + expand(1, g_down, columns)).astype(half)
+        return carry
+
+    lax.fori_loop(0, tiles, finish_forward, 0)
+    reduce_land(0, 3)
+    reduce_hop(0, 2)
+    lax.fori_loop(0, tiles, finish_backward, 0)
+    reduce_land(0, 2)
+    reduce_hop(0, 1)
+    reduce_land(0, 1)
+    reduce_end(0, grad_down)
+    for kind in (0, 1):
+        for t in (1, 2, 3):
+            sent(kind, t)
+            reduce_sent(kind, t)
+        for k in (1, 2, 3):
+            low_copy(kind, k).wait_send()
+    for copy in (dy_far, dy_near, dy_relay, near_first, near_second, far_copy):
+        copy.wait_send()
+
+
+def fused_call(x, dy, mask, down, up, w):
+    rows, width = x.shape
+    block = down.shape[0]
+    dma = pltpu.SemaphoreType.DMA
+    vmem = pl.BlockSpec(memory_space=pltpu.VMEM)
+    scratch = [
+        pltpu.VMEM((4, block, width), half),
+        pltpu.VMEM((4, block, width), half),
+        pltpu.VMEM((4, block, width), half),
+        pltpu.VMEM((4, block, width), half),
+        pltpu.VMEM((2, 3, block, width), half),
+        pltpu.VMEM((2, 3, block, width), half),
+        pltpu.VMEM((4, rows, width), half),
+        pltpu.VMEM((2, rows, width), half),
+        pltpu.VMEM((rows, width), half),
+        pltpu.VMEM((3, rows, width), half),
+        pltpu.VMEM((rows, width), f32),
+        pltpu.VMEM((2, rows, 128), f32),
+        pltpu.VMEM((2, 3, rows, 128), f32),
+        pltpu.VMEM((2, rows, 4 * block), half),
+        pltpu.VMEM((2, w.shape[0], TILE), half),
+        dma((2,)),
+        dma((2, 2, 3)),
+        dma((2, 2, 3)),
+        dma((2, 2, 3)),
+        dma((2, 2, 3)),
+        dma((6,)),
+        dma((6,)),
+        dma((2, 3)),
+        dma((2, 3)),
+    ]
+    return pl.pallas_call(
+        fused_kernel,
+        out_shape=[
+            jax.ShapeDtypeStruct((rows, width), half),
+            jax.ShapeDtypeStruct((rows, width), half),
+            jax.ShapeDtypeStruct((block, width), f32),
+            jax.ShapeDtypeStruct((block, width), f32),
+        ],
+        in_specs=[vmem] * 5 + [pl.BlockSpec(memory_space=pl.ANY)],
+        out_specs=[vmem] * 4,
+        scratch_shapes=scratch,
+        compiler_params=pltpu.CompilerParams(
+            collective_id=0, has_side_effects=True, vmem_limit_bytes=58 * 1024 * 1024
+        ),
+        cost_estimate=pl.CostEstimate(
+            flops=4 * rows * width * 4 * width, bytes_accessed=80 * 2**20, transcendentals=0
+        ),
+    )(x, dy, mask, down, up, w)
+
+
+def fits(n_tensor, n_adapter, block, width):
+    return n_tensor == 4 and n_adapter == 4 and block == 128 and width % (2 * TILE) == 0
 
 
 def make(n_tensor, n_adapter):
@@ -124,6 +463,41 @@
         count = adapter_storage_rows.shape[0]
         own, rank, width = shrink_factor_matrices.shape
         zi, ti = lax.axis_index("adapter"), lax.axis_index("tensor")
+        def finish(layer_result, input_sensitivity, grad_down, grad_up):
+            shape = shrink_factor_matrices.shape
+            p_up, m_up, v_up = optimizer_advance(
+                expand_factor_matrices,
+                grad_up.reshape(shape),
+                expand_running_mean,
+                expand_running_variance,
+            )
+            p_down, m_down, v_down = optimizer_advance(
+                shrink_factor_matrices,
+                grad_down.reshape(shape),
+                shrink_running_mean,
+                shrink_running_variance,
+            )
+            return (layer_result, input_sensitivity, p_down, p_up, m_down, m_up, v_down, v_up)
+
+        if fits(n_tensor, n_adapter, own * rank, width):
+            labels = lax.broadcasted_iota(jnp.int32, (1, count), 1)
+            stored = jnp.sum(
+                jnp.where(tenant == labels, adapter_storage_rows[None, :], 0),
+                axis=1,
+                keepdims=True,
+            )
+            place = lax.broadcasted_iota(jnp.int32, (1, count * rank), 1) // rank
+            mask = (stored == place).astype(f32)
+            layer_result, input_sensitivity, grad_down, grad_up = fused_call(
+                tokens,
+                output_gradient,
+                mask,
+                shrink_factor_matrices.reshape(own * rank, width),
+                expand_factor_matrices.reshape(own * rank, width),
+                frozen_projection_weight,
+            )
+            return finish(layer_result, input_sensitivity, grad_down, grad_up)
+
         down_own = shrink_factor_matrices.reshape(own * rank, width).astype(half)
         up_own = expand_factor_matrices.reshape(own * rank, width).astype(half)
 
@@ -177,20 +551,7 @@
         base_back = last(dy_full, frozen_projection_weight)
         input_sensitivity = (base_back + back.astype(f32)).astype(half)
 
-        shape = shrink_factor_matrices.shape
-        p_up, m_up, v_up = optimizer_advance(
-            expand_factor_matrices,
-            grad_up.reshape(shape),
-            expand_running_mean,
-            expand_running_variance,
-        )
-        p_down, m_down, v_down = optimizer_advance(
-            shrink_factor_matrices,
-            grad_down.reshape(shape),
-            shrink_running_mean,
-            shrink_running_variance,
-        )
-        return (layer_result, input_sensitivity, p_down, p_up, m_down, m_up, v_down, v_up)
+        return finish(layer_result, input_sensitivity, grad_down, grad_up)
 
     return on_device
 

time: 288 us -> 155 us (0.54)
  Pallas kernels: 0 us -> 140 us
  waiting for transfers between devices: 119 us -> 0 us
  starting transfers between devices: 64.2 us -> 0 us
  matrix products: 42.7 us -> 0 us
  local copies, waits for them, and re-layouts: 27.4 us -> 4.63 us
  other arithmetic: 29.3 us -> 7.5 us
    pallas_call x0 -> x1, Pallas kernels: none -> 140 us  [fused_call(): pl.pallas_call(fused_kernel, out_shape=[jax.ShapeDtypeStruct((rows, width...]
    ppermute x34 -> x0, waiting for transfers between devices: 119 us -> none  [the longest x6 44.1 us: chain_scatter(): lax.ppermute(rightward.astype(half), 'adapter', [(i, i + 1) for i in rang...]
    ppermute x34 -> x0, starting transfers between devices: 64.2 us -> none  [the longest x6 15.1 us: chain_gather(): lax.ppermute(left[-1], 'adapter', [(i, i + 1) for i in range(t - 1, size...]
    dot_general x8 -> x0, matrix products: 42.7 us -> none  [the longest x3 20.1 us: last(): lax.dot_general(a, b, (((1,), (1,)), ((), ())), preferred_element_type=f32)]
    dynamic_slice x2 -> x0, local copies, waits for them, and re-layouts: 16.7 us -> none  [the longest x1 13.1 us: tensor_scatter(): keep = lax.dynamic_index_in_dim(pairs, mine, 2, keepdims=False)]
    another operation x3 -> x0, local copies, waits for them, and re-layouts: 8.08 us -> none  [the longest x1 7.82 us: tensor_scatter(): pairs = total.reshape(rows, -1, 2, width)]
    add x6 -> x0, other arithmetic: 7.79 us -> none  [the longest x1 4.22 us: tensor_scatter(): total = keep.astype(f32) + other.astype(f32)]
    another operation x3 -> x0, other arithmetic: 4.02 us -> none  [tensor_gather(): jnp.stack([jnp.where(high, other, held), jnp.where(high, held, other)], a...]
  transfers between devices with their start and end apart: 34 -> 0, of which waited for: 15 -> 0; matrix products, arithmetic and copies ran while one was open for 31% -> 0% of each run, Pallas kernels for 0% -> 0%
where the time goes in v2:
time: 155 us; the launch traced here: 153 us
  Pallas kernels  140 us (90%)
  other arithmetic  7.5 us (5%)
  local copies, waits for them, and re-layouts  4.63 us (3%)
    pallas_call x1, Pallas kernels, fused_call(): pl.pallas_call(fused_kernel, out_shape=[jax.ShapeDtypeStruct((rows, width...  140 us
    sub x1, other arithmetic, optimizer_advance(): param - learn_rate * (first_next / fix_one) / (jnp.sqrt(second_next / fix...  5.67 us
    unnamed x12, local copies, waits for them, and re-layouts  4.63 us

profile of v2, /device:TPU:15, one launch (start us, length us, event | category | flops | bytes accessed | tf_op | source)
XLA Modules:
  0.0 152.7 jit_solution(17491808030391095452)
XLA Ops:
  0.6 0.0 copy-start.1
  0.6 0.0 copy-start
  0.7 0.0 copy-start.3
  0.7 0.0 copy-start.4
  0.7 0.0 copy-start.2
  0.7 0.9 select_reduce_fusion
  1.6 0.9 compare_convert_fusion.mask
  2.5 139.9 %shard_map.170 = (bf16[256,2048]{1,0:T(8,128)(2,1)}, bf16[256,2048]{1,0:T(8,128)(2,1)}, f32[128,2048]{1,0:T(8,128)}, f32[128,2048]{1,0:T(8,128)}) custom-call(bf16[256,2048]{1,0:T(8,128)(2,1)} %x.1, bf16[256,2048]{1,0:T(8,128)(2,1)} %dy.1, f32[256,512]{1,0:T(8,128)} %compare_convert_fusion.mask, f32[128,2048]{1,0:T(8,128)} %bitcast.5, f32[128,2048]{1,0:T(8,128)} %bitcast.6, ...), custom_call_target="tpu_custom_call" | custom-call | flops 17179869184 | bytes 83886080 | tf_op jit(solution)/shard_map/pallas_call | solution.py:425
  142.4 0.0 copy-done.1
  142.4 0.0 copy-done
  142.4 0.0 copy-done.3
  142.4 0.0 copy-done.4
  142.5 0.0 copy-done.2
  142.5 5.7 %divide_subtract_fusion = (f32[2,64,2048]{2,1,0:T(8,128)}, f32[2,64,2048]{2,1,0:T(8,128)}, f32[2,64,2048]{2,1,0:T(8,128)}, f32[2,64,2048]{2,1,0:T(8,128)}, f32[2,64,2048]{2,1,0:T(8,128)}, /*index=5*/f32[2,64,2048]{2,1,0:T(8,128)}) fusion(f32[2,64,2048]{2,1,0:T(8,128)S(1)} %copy-done.1, f32[2,64,2048]{2,1,0:T(8,128)} %bitcast.8, ...), kind=kLoop, calls=%fused_computation.4 | loop fusion | flops 6291456 | bytes 14680064 | tf_op jit(solution)/shard_map/sub | solution.py:23
  148.1 2.3 %copy.21 = bf16[256,2048]{1,0:T(8,128)(2,1)} copy(bf16[256,2048]{1,0:T(8,128)(2,1)} %get-tuple-element.33) | data formatting | bytes 2097152
  150.4 2.3 %copy.22 = bf16[256,2048]{1,0:T(8,128)(2,1)} copy(bf16[256,2048]{1,0:T(8,128)(2,1)} %get-tuple-element.34) | data formatting | bytes 2097152
  (1 shorter events, 0.0 us)
Async XLA Ops:
  0.6 141.8 %copy-start.1 = (f32[2,64,2048]{2,1,0:T(8,128)S(1)}, f32[2,64,2048]{2,1,0:T(8,128)}, u32[]{:S(2)}) copy-start(f32[2,64,2048]{2,1,0:T(8,128)} %param.16) | copy-start | bytes 3145732
  0.6 141.8 %copy-start = (f32[2,64,2048]{2,1,0:T(8,128)S(1)}, f32[2,64,2048]{2,1,0:T(8,128)}, u32[]{:S(2)}) copy-start(f32[2,64,2048]{2,1,0:T(8,128)} %param.15) | copy-start | bytes 3145732
  0.7 141.8 %copy-start.3 = (f32[2,64,2048]{2,1,0:T(8,128)S(1)}, f32[2,64,2048]{2,1,0:T(8,128)}, u32[]{:S(2)}) copy-start(f32[2,64,2048]{2,1,0:T(8,128)} %param.20) | copy-start | bytes 3145732
  0.7 141.8 %copy-start.4 = (f32[2,64,2048]{2,1,0:T(8,128)S(1)}, f32[2,64,2048]{2,1,0:T(8,128)}, u32[]{:S(2)}) copy-start(f32[2,64,2048]{2,1,0:T(8,128)} %param.19) | copy-start | bytes 3145732
  0.7 141.8 %copy-start.2 = (f32[2,64,2048]{2,1,0:T(8,128)S(1)}, f32[2,64,2048]{2,1,0:T(8,128)}, u32[]{:S(2)}) copy-start(f32[2,64,2048]{2,1,0:T(8,128)} %param.18) | copy-start | bytes 3145732

commit v3 on v2

--- a/solution.py
+++ b/solution.py
@@ -1,3 +1,5 @@
+import functools
+
 import jax
 import jax.numpy as jnp
 from jax import lax
@@ -122,11 +124,11 @@
 
 
 def fused_kernel(
-    x, dy, mask, down, up, w,
+    per, x, dy, tenant, ids, down, up, w,
     layer, sens, grad_down, grad_up,
     g_down, g_up, t_down, t_up, r_down, r_up,
-    part, near, far, dyg, acc, lows, low_in, spread_low,
-    wbuf, w_sem, z_send, z_recv, r_send, r_recv, y_send, y_recv, l_send, l_recv,
+    part, near, far, dyg, acc, made, mask, lows, low_in, spread_low,
+    wbuf, w_sem, z_send, z_recv, r_send, r_recv, y_send, y_recv, l_send, l_recv, out_sem,
 ):
     zi, ti = lax.axis_index("adapter"), lax.axis_index("tensor")
     nz = 4
@@ -164,10 +166,16 @@
             src_ref=src, dst_ref=dst, send_sem=send, recv_sem=recv,
             device_id={"adapter": to}, device_id_type=MESH)
 
-    def gather_copy(kind, t, direction, owner):
+    cut = down.shape[0] // 2
+
+    def rows_of(h):
+        return pl.ds(h * cut, cut)
+
+    def gather_copy(kind, t, h, direction, owner):
         g = (g_down, g_up)[kind]
-        return remote_z(g.at[owner], g.at[owner], z_send.at[kind, direction, t - 1],
-                        z_recv.at[kind, direction, t - 1], direction)
+        block = g.at[owner, rows_of(h)]
+        return remote_z(block, block, z_send.at[kind, direction, t - 1, h],
+                        z_recv.at[kind, direction, t - 1, h], direction)
 
     def may_right(t):
         return (zi < nz - 1) & (zi - t + 1 >= 0)
@@ -175,25 +183,30 @@
     def may_left(t):
         return (zi > 0) & (zi + t - 1 <= nz - 1)
 
-    def hop(kind, t):
-        when(may_right(t), lambda: gather_copy(kind, t, 0, zi - t + 1).start())
-        when(may_left(t), lambda: gather_copy(kind, t, 1, zi + t - 1).start())
-
-    def land(kind, t):
-        when(zi - t >= 0, lambda: gather_copy(kind, t, 0, zi - t).wait_recv())
-        when(zi + t <= nz - 1, lambda: gather_copy(kind, t, 1, zi + t).wait_recv())
-
-    def sent(kind, t):
-        when(may_right(t), lambda: gather_copy(kind, t, 0, zi - t + 1).wait_send())
-        when(may_left(t), lambda: gather_copy(kind, t, 1, zi + t - 1).wait_send())
-
-    def reduce_copy(kind, d, direction, owner):
+    def hop(kind, t, h):
+        when(may_right(t), lambda: gather_copy(kind, t, h, 0, zi - t + 1).start())
+        when(may_left(t), lambda: gather_copy(kind, t, h, 1, zi + t - 1).start())
+
+    def land(kind, t, h):
+        when(zi - t >= 0, lambda: gather_copy(kind, t, h, 0, zi - t).wait_recv())
+        when(zi + t <= nz - 1, lambda: gather_copy(kind, t, h, 1, zi + t).wait_recv())
+
+    def sent(kind, t, h):
+        when(may_right(t), lambda: gather_copy(kind, t, h, 0, zi - t + 1).wait_send())
+        when(may_left(t), lambda: gather_copy(kind, t, h, 1, zi + t - 1).wait_send())
+
+    def relay(kind, t):
+        for h in (0, 1):
+            land(kind, t, h)
+            hop(kind, t + 1, h)
+
+    def reduce_copy(kind, d, h, direction, owner):
         terms, arrived = ((t_down, r_down), (t_up, r_up))[kind]
-        return remote_z(terms.at[owner], arrived.at[direction, d - 1],
-                        r_send.at[kind, direction, d - 1], r_recv.at[kind, direction, d - 1],
-                        direction)
-
-    def reduce_hop(kind, d):
+        return remote_z(terms.at[owner, rows_of(h)], arrived.at[direction, d - 1, rows_of(h)],
+                        r_send.at[kind, direction, d - 1, h],
+                        r_recv.at[kind, direction, d - 1, h], direction)
+
+    def reduce_hop(kind, d, h):
         terms, arrived = ((t_down, r_down), (t_up, r_up))[kind]
 
         def go(direction):
@@ -202,27 +215,33 @@
             def fn():
                 if d < nz - 1:
                     def add():
-                        terms[owner] = (
-                            terms[owner].astype(f32) + arrived[direction, d].astype(f32)
+                        terms[owner, rows_of(h)] = (
+                            terms[owner, rows_of(h)].astype(f32)
+                            + arrived[direction, d, rows_of(h)].astype(f32)
                         ).astype(half)
 
                     when(zi > 0 if direction == 0 else zi < nz - 1, add)
-                reduce_copy(kind, d, direction, owner).start()
+                reduce_copy(kind, d, h, direction, owner).start()
 
             return fn
 
         when(zi + d <= nz - 1, go(0))
         when(zi - d >= 0, go(1))
 
-    def reduce_land(kind, d):
+    def reduce_land(kind, d, h):
         when((zi > 0) & (zi - 1 + d <= nz - 1),
-             lambda: reduce_copy(kind, d, 0, 0).wait_recv())
+             lambda: reduce_copy(kind, d, h, 0, 0).wait_recv())
         when((zi < nz - 1) & (zi + 1 - d >= 0),
-             lambda: reduce_copy(kind, d, 1, 0).wait_recv())
-
-    def reduce_sent(kind, d):
-        when(zi + d <= nz - 1, lambda: reduce_copy(kind, d, 0, zi + d).wait_send())
-        when(zi - d >= 0, lambda: reduce_copy(kind, d, 1, zi - d).wait_send())
+             lambda: reduce_copy(kind, d, h, 1, 0).wait_recv())
+
+    def reduce_sent(kind, d, h):
+        when(zi + d <= nz - 1, lambda: reduce_copy(kind, d, h, 0, zi + d).wait_send())
+        when(zi - d >= 0, lambda: reduce_copy(kind, d, h, 1, zi - d).wait_send())
+
+    def reduce_relay(kind, d):
+        for h in (0, 1):
+            reduce_land(kind, d, h)
+            reduce_hop(kind, d - 1, h)
 
     def reduce_end(kind, out):
         terms, arrived = ((t_down, r_down), (t_up, r_up))[kind]
@@ -314,50 +333,52 @@
                              preferred_element_type=f32)
         return total.astype(half).astype(f32)
 
-    hop(0, 1)
+    hop(0, 1, 0)
+    hop(0, 1, 1)
     dy_far.start()
     dy_near.start()
     acc[...] = jnp.zeros_like(acc)
+    lanes = lax.broadcasted_iota(jnp.int32, (1, ids.shape[1]), 1)
+    stored = jnp.sum(jnp.where(tenant[...] == lanes, ids[...], 0.0), axis=1, keepdims=True)
+    places = (lax.broadcasted_iota(jnp.int32, (1, nz * 128), 1) // (128 // per)).astype(f32)
+    mask[...] = jnp.where(stored == places, 1.0, 0.0)
     forward(0)
     near_first.start()
     forward(1)
     near_first.wait_recv()
     part[2] = (part[2].astype(f32) + near[0].astype(f32)).astype(half)
     far_copy.start()
-    land(0, 1)
-    hop(0, 2)
+    relay(0, 1)
     forward(2)
     near_second.start()
     forward(3)
-    land(0, 2)
-    hop(0, 3)
+    relay(0, 2)
+    hop(1, 1, 0)
     dy_far.wait_recv()
     dy_relay.start()
     backward(4)
-    land(0, 3)
-    hop(1, 1)
+    land(0, 3, 0)
+    land(0, 3, 1)
+    hop(1, 1, 1)
     low_start(0, x, g_down)
     dy_near.wait_recv()
     low_end(0, dy, t_up)
-    reduce_hop(1, 3)
+    reduce_hop(1, 3, 0)
+    reduce_hop(1, 3, 1)
     backward(5)
-    land(1, 1)
-    hop(1, 2)
-    reduce_land(1, 3)
-    reduce_hop(1, 2)
+    relay(1, 1)
+    reduce_relay(1, 3)
     backward(6)
-    land(1, 2)
-    hop(1, 3)
-    reduce_land(1, 2)
-    reduce_hop(1, 1)
+    relay(1, 2)
+    reduce_relay(1, 2)
     dy_relay.wait_recv()
     backward(7)
-    land(1, 3)
+    land(1, 3, 0)
+    land(1, 3, 1)
     low_start(1, dy, g_up)
     low_end(1, x, t_down)
-    reduce_hop(0, 3)
-    reduce_land(1, 1)
-    reduce_end(1, grad_up)
+    reduce_hop(0, 3, 0)
+    reduce_hop(0, 3, 1)
     near_second.wait_recv()
     far_copy.wait_recv()
 
@@ -365,35 +386,45 @@
         columns = pl.ds(pl.multiple_of(j * TILE, TILE), TILE)
         base = part[0, :, columns].astype(f32) + near[1, :, columns].astype(f32)
         base = base + far[:, columns].astype(f32)
-        layer[:, columns] = (base + expand(0, g_up, columns)).astype(half)
+        made[:, columns] = base + expand(0, g_up, columns)
         return carry
 
     def finish_backward(j, carry):
         columns = pl.ds(pl.multiple_of(j * TILE, TILE), TILE)
-        sens[:, columns] = (acc[:, columns] + expand(1, g_down, columns)).astype(half)
+        acc[:, columns] += expand(1, g_down, columns)
         return carry
 
     lax.fori_loop(0, tiles, finish_forward, 0)
-    reduce_land(0, 3)
-    reduce_hop(0, 2)
+    layer_out = pltpu.make_async_copy(made, layer, out_sem.at[0])
+    layer_out.start()
+    reduce_relay(0, 3)
     lax.fori_loop(0, tiles, finish_backward, 0)
-    reduce_land(0, 2)
-    reduce_hop(0, 1)
-    reduce_land(0, 1)
+    sens_out = pltpu.make_async_copy(acc, sens, out_sem.at[1])
+    sens_out.start()
+    reduce_land(1, 1, 0)
+    reduce_land(1, 1, 1)
+    reduce_end(1, grad_up)
+    reduce_relay(0, 2)
+    reduce_land(0, 1, 0)
+    reduce_land(0, 1, 1)
     reduce_end(0, grad_down)
+    layer_out.wait()
+    sens_out.wait()
     for kind in (0, 1):
         for t in (1, 2, 3):
-            sent(kind, t)
-            reduce_sent(kind, t)
+            for h in (0, 1):
+                sent(kind, t, h)
+                reduce_sent(kind, t, h)
         for k in (1, 2, 3):
             low_copy(kind, k).wait_send()
     for copy in (dy_far, dy_near, dy_relay, near_first, near_second, far_copy):
         copy.wait_send()
 
 
-def fused_call(x, dy, mask, down, up, w):
+def fused_call(x, dy, tenant, ids, down, up, w):
     rows, width = x.shape
     block = down.shape[0]
+    per = ids.shape[1] // 4
     dma = pltpu.SemaphoreType.DMA
     vmem = pl.BlockSpec(memory_space=pltpu.VMEM)
     scratch = [
@@ -408,30 +439,33 @@
         pltpu.VMEM((rows, width), half),
         pltpu.VMEM((3, rows, width), half),
         pltpu.VMEM((rows, width), f32),
+        pltpu.VMEM((rows, width), f32),
+        pltpu.VMEM((rows, 4 * block), f32),
         pltpu.VMEM((2, rows, 128), f32),
         pltpu.VMEM((2, 3, rows, 128), f32),
         pltpu.VMEM((2, rows, 4 * block), half),
         pltpu.VMEM((2, w.shape[0], TILE), half),
         dma((2,)),
-        dma((2, 2, 3)),
-        dma((2, 2, 3)),
-        dma((2, 2, 3)),
-        dma((2, 2, 3)),
+        dma((2, 2, 3, 2)),
+        dma((2, 2, 3, 2)),
+        dma((2, 2, 3, 2)),
+        dma((2, 2, 3, 2)),
         dma((6,)),
         dma((6,)),
         dma((2, 3)),
         dma((2, 3)),
+        dma((2,)),
     ]
     return pl.pallas_call(
-        fused_kernel,
+        functools.partial(fused_kernel, per),
         out_shape=[
-            jax.ShapeDtypeStruct((rows, width), half),
-            jax.ShapeDtypeStruct((rows, width), half),
+            jax.ShapeDtypeStruct((rows, width), f32),
+            jax.ShapeDtypeStruct((rows, width), f32),
             jax.ShapeDtypeStruct((block, width), f32),
             jax.ShapeDtypeStruct((block, width), f32),
         ],
-        in_specs=[vmem] * 5 + [pl.BlockSpec(memory_space=pl.ANY)],
-        out_specs=[vmem] * 4,
+        in_specs=[vmem] * 6 + [pl.BlockSpec(memory_space=pl.ANY)],
+        out_specs=[pl.BlockSpec(memory_space=pl.ANY)] * 2 + [vmem] * 2,
         scratch_shapes=scratch,
         compiler_params=pltpu.CompilerParams(
             collective_id=0, has_side_effects=True, vmem_limit_bytes=58 * 1024 * 1024
@@ -439,7 +473,7 @@
         cost_estimate=pl.CostEstimate(
             flops=4 * rows * width * 4 * width, bytes_accessed=80 * 2**20, transcendentals=0
         ),
-    )(x, dy, mask, down, up, w)
+    )(x, dy, tenant, ids, down, up, w)
 
 
 def fits(n_tensor, n_adapter, block, width):
@@ -480,23 +514,18 @@
             return (layer_result, input_sensitivity, p_down, p_up, m_down, m_up, v_down, v_up)
 
         if fits(n_tensor, n_adapter, own * rank, width):
-            labels = lax.broadcasted_iota(jnp.int32, (1, count), 1)
-            stored = jnp.sum(
-                jnp.where(tenant == labels, adapter_storage_rows[None, :], 0),
-                axis=1,
-                keepdims=True,
-            )
-            place = lax.broadcasted_iota(jnp.int32, (1, count * rank), 1) // rank
-            mask = (stored == place).astype(f32)
             layer_result, input_sensitivity, grad_down, grad_up = fused_call(
                 tokens,
                 output_gradient,
-                mask,
+                tenant,
+                adapter_storage_rows.astype(f32).reshape(1, count),
                 shrink_factor_matrices.reshape(own * rank, width),
                 expand_factor_matrices.reshape(own * rank, width),
                 frozen_projection_weight,
             )
-            return finish(layer_result, input_sensitivity, grad_down, grad_up)
+            return finish(
+                layer_result.astype(half), input_sensitivity.astype(half), grad_down, grad_up
+            )
 
         down_own = shrink_factor_matrices.reshape(own * rank, width).astype(half)
         up_own = expand_factor_matrices.reshape(own * rank, width).astype(half)

time: 155 us -> 151 us (0.974)
  Pallas kernels: 140 us -> 136 us
  other arithmetic: 7.5 us -> 10.5 us
  local copies, waits for them, and re-layouts: 4.63 us -> 2.59 us
    pallas_call x1, Pallas kernels: 140 us -> 136 us  [fused_call(): pl.pallas_call(functools.partial(fused_kernel, per), out_shape=[jax.Shape...]
    convert_element_type x1 -> x2, other arithmetic: 0.9 us -> 3.98 us  [the longest x1 2.86 us: on_device(): layer_result.astype(half)]
    unnamed x12 -> x15, local copies, waits for them, and re-layouts: 4.63 us -> 2.59 us
where the time goes in v3:
time: 151 us; the launch traced here: 150 us
  Pallas kernels  136 us (90%)
  other arithmetic  10.5 us (7%)
  local copies, waits for them, and re-layouts  2.59 us (2%)
    pallas_call x1, Pallas kernels, fused_call(): pl.pallas_call(functools.partial(fused_kernel, per), out_shape=[jax.Shape...  136 us
    sub x1, other arithmetic, optimizer_advance(): param - learn_rate * (first_next / fix_one) / (jnp.sqrt(second_next / fix...  5.35 us

profile of v3, /device:TPU:15, one launch (start us, length us, event | category | flops | bytes accessed | tf_op | source)
XLA Modules:
  0.0 149.9 jit_solution(3625348225699001922)
XLA Ops:
  0.6 1.2 convert_bitcast_fusion.ids
  1.8 1.5 copy.19.tenant
  3.3 0.0 copy-start.5
  3.3 0.0 copy-start.6
  3.3 136.2 %shard_map.170 = (f32[256,2048]{1,0:T(8,128)}, f32[256,2048]{1,0:T(8,128)}, f32[128,2048]{1,0:T(8,128)}, f32[128,2048]{1,0:T(8,128)}) custom-call(bf16[256,2048]{1,0:T(8,128)(2,1)} %x.1, bf16[256,2048]{1,0:T(8,128)(2,1)} %dy.1, s32[256,1]{1,0:T(8,128)} %copy.19.tenant, f32[1,8]{1,0:T(1,128)} %convert_bitcast_fusion.ids, f32[128,2048]{1,0:T(8,128)} %bitcast.6, ...), custom_call_target="tpu_custom_call" | custom-call | flops 17179869184 | bytes 83886080 | tf_op jit(solution)/shard_map/pallas_call | solution.py:459
  139.4 0.0 copy-start
  139.5 0.0 copy-start.4
  139.5 2.9 %convert_element_type.10 = bf16[256,2048]{1,0:T(8,128)(2,1)} convert(f32[256,2048]{1,0:T(8,128)} %get-tuple-element.12) | non-fusion elementwise | flops 524288 | bytes 3145728 | tf_op jit(solution)/shard_map/convert_element_type | solution.py:527
  142.3 0.0 copy-done
  142.3 0.0 copy-start.1
  142.3 0.0 copy-start.2
  142.3 0.0 copy-start.3
  142.3 1.1 convert_element_type.11
  143.5 0.0 copy-done.5
  143.5 0.0 copy-done.6
  143.5 0.0 copy-done.4
  143.5 0.4 copy-done.1
  143.9 0.3 copy-done.2
  144.3 0.3 copy-done.3
  144.6 5.4 %divide_subtract_fusion = (f32[2,64,2048]{2,1,0:T(8,128)}, f32[2,64,2048]{2,1,0:T(8,128)}, f32[2,64,2048]{2,1,0:T(8,128)}, f32[2,64,2048]{2,1,0:T(8,128)}, f32[2,64,2048]{2,1,0:T(8,128)}, /*index=5*/f32[2,64,2048]{2,1,0:T(8,128)}) fusion(f32[2,64,2048]{2,1,0:T(8,128)S(1)} %copy-done.2, f32[2,64,2048]{2,1,0:T(8,128)} %bitcast.9, ...), kind=kLoop, calls=%fused_computation.4 | loop fusion | flops 6291456 | bytes 14680064 | tf_op jit(solution)/shard_map/sub | solution.py:25
Async XLA Ops:
  3.3 140.2 %copy-start.5 = (f32[2,64,2048]{2,1,0:T(8,128)S(1)}, f32[2,64,2048]{2,1,0:T(8,128)}, u32[]{:S(2)}) copy-start(f32[2,64,2048]{2,1,0:T(8,128)} %param.19) | copy-start | bytes 3145732
  3.3 140.2 %copy-start.6 = (f32[2,64,2048]{2,1,0:T(8,128)S(1)}, f32[2,64,2048]{2,1,0:T(8,128)}, u32[]{:S(2)}) copy-start(f32[2,64,2048]{2,1,0:T(8,128)} %param.17) | copy-start | bytes 3145732
  139.4 2.9 %copy-start = (f32[256,2048]{1,0:T(8,128)S(1)}, f32[256,2048]{1,0:T(8,128)}, u32[]{:S(2)}) copy-start(f32[256,2048]{1,0:T(8,128)} %get-tuple-element.13) | copy-start | bytes 6291460
  139.5 4.0 %copy-start.4 = (f32[2,64,2048]{2,1,0:T(8,128)S(1)}, f32[2,64,2048]{2,1,0:T(8,128)}, u32[]{:S(2)}) copy-start(f32[2,64,2048]{2,1,0:T(8,128)} %param.20) | copy-start | bytes 3145732
  142.3 1.6 %copy-start.1 = (f32[2,64,2048]{2,1,0:T(8,128)S(1)}, f32[2,64,2048]{2,1,0:T(8,128)}, u32[]{:S(2)}) copy-start(f32[2,64,2048]{2,1,0:T(8,128)} %param.15) | copy-start | bytes 3145732
  142.3 1.9 %copy-start.2 = (f32[2,64,2048]{2,1,0:T(8,128)S(1)}, f32[2,64,2048]{2,1,0:T(8,128)}, u32[]{:S(2)}) copy-start(f32[2,64,2048]{2,1,0:T(8,128)} %param.16) | copy-start | bytes 3145732
  142.3 2.2 %copy-start.3 = (f32[2,64,2048]{2,1,0:T(8,128)S(1)}, f32[2,64,2048]{2,1,0:T(8,128)}, u32[]{:S(2)}) copy-start(f32[2,64,2048]{2,1,0:T(8,128)} %param.18) | copy-start | bytes 3145732

commit v4 on v3

--- a/solution.py
+++ b/solution.py
@@ -147,7 +147,6 @@
     for k in (1, 2, 3):
         pl.semaphore_signal(barrier, inc=1, device_id={"tensor": peers[k]}, device_id_type=MESH)
     g_down[zi] = down[...].astype(half)
-    g_up[zi] = up[...].astype(half)
 
     order = [3, 2, 1, 0, 0, 1, 2, 3]
 
@@ -337,6 +336,7 @@
     hop(0, 1, 1)
     dy_far.start()
     dy_near.start()
+    g_up[zi] = up[...].astype(half)
     acc[...] = jnp.zeros_like(acc)
     lanes = lax.broadcasted_iota(jnp.int32, (1, ids.shape[1]), 1)
     stored = jnp.sum(jnp.where(tenant[...] == lanes, ids[...], 0.0), axis=1, keepdims=True)
@@ -354,19 +354,19 @@
     forward(3)
     relay(0, 2)
     hop(1, 1, 0)
+    hop(1, 1, 1)
     dy_far.wait_recv()
     dy_relay.start()
     backward(4)
     land(0, 3, 0)
     land(0, 3, 1)
-    hop(1, 1, 1)
     low_start(0, x, g_down)
     dy_near.wait_recv()
     low_end(0, dy, t_up)
     reduce_hop(1, 3, 0)
     reduce_hop(1, 3, 1)
+    relay(1, 1)
     backward(5)
-    relay(1, 1)
     reduce_relay(1, 3)
     backward(6)
     relay(1, 2)

time: 151 us -> 151 us (level)
  no operation moved by 1% of the time
where the time goes in v4:
time: 151 us; the launch traced here: 150 us
  Pallas kernels  136 us (90%)
  other arithmetic  10.5 us (7%)
  local copies, waits for them, and re-layouts  2.59 us (2%)
    pallas_call x1, Pallas kernels, fused_call(): pl.pallas_call(functools.partial(fused_kernel, per), out_shape=[jax.Shape...  136 us
    sub x1, other arithmetic, optimizer_advance(): param - learn_rate * (first_next / fix_one) / (jnp.sqrt(second_next / fix...  5.35 us

profile of v4, /device:TPU:15, one launch (start us, length us, event | category | flops | bytes accessed | tf_op | source)
XLA Modules:
  0.0 149.9 jit_solution(9869629710331890306)
XLA Ops:
  0.6 1.2 convert_bitcast_fusion.ids
  1.8 1.5 copy.19.tenant
  3.3 0.0 copy-start.5
  3.3 0.0 copy-start.6
  3.3 136.1 %shard_map.170 = (f32[256,2048]{1,0:T(8,128)}, f32[256,2048]{1,0:T(8,128)}, f32[128,2048]{1,0:T(8,128)}, f32[128,2048]{1,0:T(8,128)}) custom-call(bf16[256,2048]{1,0:T(8,128)(2,1)} %x.1, bf16[256,2048]{1,0:T(8,128)(2,1)} %dy.1, s32[256,1]{1,0:T(8,128)} %copy.19.tenant, f32[1,8]{1,0:T(1,128)} %convert_bitcast_fusion.ids, f32[128,2048]{1,0:T(8,128)} %bitcast.6, ...), custom_call_target="tpu_custom_call" | custom-call | flops 17179869184 | bytes 83886080 | tf_op jit(solution)/shard_map/pallas_call | solution.py:459
  139.4 0.0 copy-start
  139.4 0.0 copy-start.4
  139.4 2.9 %convert_element_type.10 = bf16[256,2048]{1,0:T(8,128)(2,1)} convert(f32[256,2048]{1,0:T(8,128)} %get-tuple-element.12) | non-fusion elementwise | flops 524288 | bytes 3145728 | tf_op jit(solution)/shard_map/convert_element_type | solution.py:527
  142.3 0.0 copy-done
  142.3 0.0 copy-start.1
  142.3 0.0 copy-start.2
  142.3 0.0 copy-start.3
  142.3 1.1 convert_element_type.11
  143.4 0.0 copy-done.5
  143.4 0.0 copy-done.6
  143.5 0.0 copy-done.4
  143.5 0.4 copy-done.1
  143.9 0.3 copy-done.2
  144.2 0.3 copy-done.3
  144.6 5.4 %divide_subtract_fusion = (f32[2,64,2048]{2,1,0:T(8,128)}, f32[2,64,2048]{2,1,0:T(8,128)}, f32[2,64,2048]{2,1,0:T(8,128)}, f32[2,64,2048]{2,1,0:T(8,128)}, f32[2,64,2048]{2,1,0:T(8,128)}, /*index=5*/f32[2,64,2048]{2,1,0:T(8,128)}) fusion(f32[2,64,2048]{2,1,0:T(8,128)S(1)} %copy-done.2, f32[2,64,2048]{2,1,0:T(8,128)} %bitcast.9, ...), kind=kLoop, calls=%fused_computation.4 | loop fusion | flops 6291456 | bytes 14680064 | tf_op jit(solution)/shard_map/sub | solution.py:25
Async XLA Ops:
  3.3 140.2 %copy-start.5 = (f32[2,64,2048]{2,1,0:T(8,128)S(1)}, f32[2,64,2048]{2,1,0:T(8,128)}, u32[]{:S(2)}) copy-start(f32[2,64,2048]{2,1,0:T(8,128)} %param.19) | copy-start | bytes 3145732
  3.3 140.2 %copy-start.6 = (f32[2,64,2048]{2,1,0:T(8,128)S(1)}, f32[2,64,2048]{2,1,0:T(8,128)}, u32[]{:S(2)}) copy-start(f32[2,64,2048]{2,1,0:T(8,128)} %param.17) | copy-start | bytes 3145732
  139.4 2.9 %copy-start = (f32[256,2048]{1,0:T(8,128)S(1)}, f32[256,2048]{1,0:T(8,128)}, u32[]{:S(2)}) copy-start(f32[256,2048]{1,0:T(8,128)} %get-tuple-element.13) | copy-start | bytes 6291460
  139.4 4.0 %copy-start.4 = (f32[2,64,2048]{2,1,0:T(8,128)S(1)}, f32[2,64,2048]{2,1,0:T(8,128)}, u32[]{:S(2)}) copy-start(f32[2,64,2048]{2,1,0:T(8,128)} %param.20) | copy-start | bytes 3145732
  142.3 1.6 %copy-start.1 = (f32[2,64,2048]{2,1,0:T(8,128)S(1)}, f32[2,64,2048]{2,1,0:T(8,128)}, u32[]{:S(2)}) copy-start(f32[2,64,2048]{2,1,0:T(8,128)} %param.15) | copy-start | bytes 3145732
  142.3 1.9 %copy-start.2 = (f32[2,64,2048]{2,1,0:T(8,128)S(1)}, f32[2,64,2048]{2,1,0:T(8,128)}, u32[]{:S(2)}) copy-start(f32[2,64,2048]{2,1,0:T(8,128)} %param.16) | copy-start | bytes 3145732
  142.3 2.2 %copy-start.3 = (f32[2,64,2048]{2,1,0:T(8,128)S(1)}, f32[2,64,2048]{2,1,0:T(8,128)}, u32[]{:S(2)}) copy-start(f32[2,64,2048]{2,1,0:T(8,128)} %param.18) | copy-start | bytes 3145732
